TPU v7x, 256 devices: a whole 4x4x8 slice. The times are simulated.
256 devices in a mesh: seq: 64 (over x, z, core), head: 4 (over y).
Axes of the slice: x: 4, y: 4, z: 8, core: 2. Of those that a mesh axis runs over, the one named last changes fastest.
Arguments:
- query_input: bfloat16 [16384, 2048], P('seq', 'head'), may hold values from -6 to 6
- key_input: bfloat16 [16384, 2048], P('seq', 'head'), may hold values from -6 to 6
- value_input: bfloat16 [16384, 2048], P('seq', 'head'), may hold values from -6 to 6
- out_weight: bfloat16 [4096, 2048], P('seq', 'head'), may hold values from -0.125 to 0.125
- cotangent: bfloat16 [16384, 4096], P('seq', 'head'), may hold values from -16 to 16
Outputs:
- layer_out: bfloat16 [16384, 4096], P('seq', 'head')
- query_grad: bfloat16 [16384, 2048], P('seq', 'head')
- key_grad: bfloat16 [16384, 2048], P('seq', 'head')
- value_grad: bfloat16 [16384, 2048], P('seq', 'head')
- weight_grad: float32 [4096, 2048], P('seq', 'head')
All inputs are finite; a program needn't handle non-finite values.
Results may differ from a plain program's by a relative error of at most 0.018.
Values may be sent and summed in bfloat16 or wider, within the bound.
A program may use at most 128 MiB of HBM per device.

v0:
```python
import jax
import jax.numpy as jnp
from jax import lax
from jax.sharding import Mesh
from jax.sharding import PartitionSpec as P

HEAD_DIM = 128
SEQ = ("seq_0", "seq_1", "seq_2")


highest = lax.Precision.HIGHEST
epsilon = 1e-06


def filled_with(x, identity):
    return jnp.zeros_like(x) + jnp.asarray(identity, x.dtype)


def entering(x, axes, combine, identity, reverse):
    before = start = filled_with(x, identity)
    running = x
    for axis in reversed(axes):
        peers, place = (lax.axis_size(axis), lax.axis_index(axis))
        pieces = lax.all_gather(running.astype(jnp.bfloat16), axis)
        inside, running = (start, start)
        for k in reversed(range(peers)) if reverse else range(peers):
            passed = k > place if reverse else k < place
            running = combine(running, pieces[k].astype(x.dtype))
            inside = jnp.where(passed, running, inside)
        before = combine(inside, before)
    return before


def from_everyone(x, axis):
    peers = lax.axis_size(axis)
    return lax.all_to_all(jnp.broadcast_to(x[None], (peers, *x.shape)), axis, 0, 0, tiled=True)


def joined_along(parts, dim):
    dims = list(parts.shape[1:])
    dims[dim] *= parts.shape[0]
    return jnp.moveaxis(parts, 0, dim).reshape(dims)


def collect(x, axis, dim):
    parts = from_everyone(x, axis)
    return joined_along(parts, dim)


def gather_in_order(x, axes, sequence):
    parts = x
    for k in sequence:
        parts = lax.all_gather(parts, axes[k])
    done = sequence[::-1]
    back = [done.index(k) for k in range(len(axes))]
    parts = parts.transpose(*back, *range(len(axes), parts.ndim))
    return parts.reshape(-1, *x.shape)


def gather_axes(x, axes, sequence, dim):
    return joined_along(gather_in_order(x, axes, sequence), dim)


def cut_along(x, dim, peers):
    dims = x.shape
    parts = x.reshape(*dims[:dim], peers, dims[dim] // peers, *dims[dim + 1 :])
    return jnp.moveaxis(parts, dim, 0)


def summed_on_arrival(x, axis, dim):
    peers = lax.axis_size(axis)
    parts = lax.all_to_all(cut_along(x, dim, peers), axis, 0, 0, tiled=True)
    return jnp.sum(parts.astype(jnp.float32), axis=0)


def features(raw_input):
    values = raw_input.astype(jnp.float32)
    return jnp.where(values > 0, values + 1.0, jnp.exp(jnp.minimum(values, 0.0)))


def feature_slope(raw_input):
    values = raw_input.astype(jnp.float32)
    return jnp.where(values > 0, 1.0, jnp.exp(jnp.minimum(values, 0.0)))


def add_states(earlier, later):
    return earlier + later


def shards(query_input, key_input, value_input, out_weight, cotangent):
    row_count = query_input.shape[0]
    local_width = query_input.shape[1]
    heads_here = local_width // HEAD_DIM
    block_rows = min(512, row_count)
    block_count = row_count // block_rows
    f32 = jnp.float32

    def split_heads(tensor_in):
        return tensor_in.reshape(block_count, block_rows, heads_here, HEAD_DIM)

    q_feat = split_heads(features(query_input).astype(jnp.bfloat16))
    k_feat = split_heads(features(key_input).astype(jnp.bfloat16))
    v_vals = split_heads(value_input)
    block_states = jnp.einsum("bthe,bthf->bhef", k_feat, v_vals, preferred_element_type=f32)
    own_state = jnp.sum(block_states, axis=0)
    prefix = entering(own_state, SEQ, add_states, jnp.zeros_like(own_state), False)
    prior_state = prefix[None] + jnp.cumsum(block_states, axis=0) - block_states
    causal = jnp.tril(jnp.ones((block_rows, block_rows), f32))
    scores = (
        jnp.einsum("bthe,bshe->bhts", q_feat, k_feat, preferred_element_type=f32) * causal
    ).astype(jnp.bfloat16)
    attended = jnp.einsum("bhts,bshf->bthf", scores, v_vals, preferred_element_type=f32)
    attended = attended + jnp.einsum(
        "bthe,bhef->bthf", q_feat.astype(f32), prior_state, precision=highest
    )
    inv_rms = lax.rsqrt(jnp.mean(attended * attended, axis=-1, keepdims=True) + epsilon)
    unit_rms = attended * inv_rms
    normed = unit_rms.reshape(row_count, local_width).astype(jnp.bfloat16)
    dy_whole = collect(cotangent, "head", 1)
    whole_weight = gather_axes(out_weight, SEQ, (0, 1, 2), 0)
    partial_value = lax.dot_general(
        normed, whole_weight, (((1,), (1,)), ((), ())), preferred_element_type=f32
    )
    upstream = jnp.dot(dy_whole, whole_weight, preferred_element_type=f32)
    layer_out = summed_on_arrival(partial_value.astype(jnp.bfloat16), "head", 1).astype(
        jnp.bfloat16
    )
    grad_scale = (row_count * lax.axis_size(SEQ)) ** (-0.5)
    weight_grad = (
        lax.psum_scatter(
            lax.dot_general(dy_whole, normed, (((0,), (0,)), ((), ())), preferred_element_type=f32),
            SEQ,
            scatter_dimension=0,
            tiled=True,
        )
        * grad_scale
    )
    d_unit = split_heads(upstream)
    inner_term = jnp.mean(d_unit * unit_rms, axis=-1, keepdims=True)
    d_att = (inv_rms * (d_unit - unit_rms * inner_term)).astype(jnp.bfloat16)
    block_adjoint = jnp.einsum("bthe,bthf->bhef", q_feat, d_att, preferred_element_type=f32)
    own_adjoint = jnp.sum(block_adjoint, axis=0)
    suffix = entering(own_adjoint, SEQ, add_states, jnp.zeros_like(own_adjoint), True)
    after_state = suffix[None] + own_adjoint[None] - jnp.cumsum(block_adjoint, axis=0)
    d_scores = (
        jnp.einsum("bthf,bshf->bhts", d_att, v_vals, preferred_element_type=f32) * causal
    ).astype(jnp.bfloat16)
    q_grad = jnp.einsum("bhts,bshe->bthe", d_scores, k_feat, preferred_element_type=f32)
    q_grad = q_grad + jnp.einsum(
        "bhef,bthf->bthe", prior_state, d_att.astype(f32), precision=highest
    )
    k_grad = jnp.einsum("bhts,bthe->bshe", d_scores, q_feat, preferred_element_type=f32)
    k_grad = k_grad + jnp.einsum(
        "bhef,bshf->bshe", after_state, v_vals.astype(f32), precision=highest
    )
    v_grad = jnp.einsum("bhts,bthf->bshf", scores, d_att, preferred_element_type=f32)
    v_grad = v_grad + jnp.einsum(
        "bhef,bshe->bshf", after_state, k_feat.astype(f32), precision=highest
    )
    query_grad = (
        (q_grad * split_heads(feature_slope(query_input)))
        .reshape(row_count, local_width)
        .astype(jnp.bfloat16)
    )
    key_grad = (
        (k_grad * split_heads(feature_slope(key_input)))
        .reshape(row_count, local_width)
        .astype(jnp.bfloat16)
    )
    value_grad = v_grad.reshape(row_count, local_width).astype(jnp.bfloat16)
    return (layer_out, query_grad, key_grad, value_grad, weight_grad)


def solution(mesh):
    split = Mesh(
        mesh.devices.reshape(4, 8, 2, mesh.shape["head"]), ("seq_0", "seq_1", "seq_2", "head")
    )
    placed = (P(SEQ, "head"), P(SEQ, "head"), P(SEQ, "head"), P(SEQ, "head"), P(SEQ, "head"))
    return jax.shard_map(
        shards,
        mesh=split,
        in_specs=placed,
        out_specs=(P(SEQ, "head"), P(SEQ, "head"), P(SEQ, "head"), P(SEQ, "head"), P(SEQ, "head")),
        check_vma=False,
    )
```

profile of v0, /device:TPU:1, one launch (start us, length us, event | category | flops | bytes accessed | tf_op | source)
XLA Modules:
  0.0 342.8 jit_solution(1054353920516948760)
XLA Ops:
  7.2 12.5 %all-gather.1 = bf16[256,512]{1,0:T(8,128)(2,1)} all-gather(bf16[64,512]{1,0:T(8,128)(2,1)} %param.8), channel_id=3, replica_groups=mesh['seq_0'=4,'seq_1'=8,'seq_2'=2,'head'=4] {'seq_0'}, dimensions={0}, use_global_device_ids=true | all-gather | bytes 327680 | tf_op jit(solution)/shard_map/all_gather | solution.py:53
  19.8 1.9 fusion.18
  22.9 5.9 %all-gather = bf16[8,128,128]{2,1,0:T(8,128)(2,1)S(1)} all-gather(bf16[4,128,128]{2,1,0:T(8,128)(2,1)S(1)} %get-tuple-element.27), channel_id=2, replica_groups=mesh['seq_0'=4,'seq_1'=8,'seq_2'=2,'head'=4] {'seq_2'}, dimensions={0}, use_global_device_ids=true | all-gather | bytes 393216 | tf_op jit(solution)/shard_map/all_gather | solution.py:24
  29.6 32.1 %all-gather.14.cloned.1.call-done = bf16[32,64,512]{2,1,0:T(8,128)(2,1)} async-done(((bf16[4,64,512]{2,1,0:T(8,128)(2,1)}), bf16[32,64,512]{2,1,0:T(8,128)(2,1)}) %all-gather.14.cloned.1.call-update) | async-done | bytes 2097168 | tf_op jit(solution)/shard_map/all_gather | solution.py:53
  61.7 1.7 broadcast_in_dim.12
  63.4 4.1 %all-to-all-start.1 = ((bf16[4,256,1024]{2,1,0:T(8,128)(2,1)}), bf16[4,256,1024]{2,1,0:T(8,128)(2,1)S(1)}, u32[]{:S(2)}, u32[]{:S(2)}) async-start(bf16[4,256,1024]{2,1,0:T(8,128)(2,1)} %broadcast_in_dim.12), calls=%async_computation.1 | async-start | bytes 4194304 | tf_op jit(solution)/shard_map/all_to_all | solution.py:36
  70.5 18.8 %all-to-all-done.1 = bf16[4,256,1024]{2,1,0:T(8,128)(2,1)S(1)} async-done(((bf16[4,256,1024]{2,1,0:T(8,128)(2,1)}), bf16[4,256,1024]{2,1,0:T(8,128)(2,1)S(1)}, u32[]{:S(2)}, u32[]{:S(2)}) %all-to-all-start.1) | async-done | bytes 2097184 | tf_op jit(solution)/shard_map/all_to_all | solution.py:36
  89.2 3.0 copy.67
  92.2 4.5 %reshape.325 = bf16[256,4096,1]{1,0,2:T(8,128)(2,1)} reshape(bf16[256,4,1024]{2,1,0:T(4,128)(2,1)} %copy.67) | data formatting | bytes 4194304 | tf_op jit(solution)/shard_map/reshape.102
  96.7 4.1 %all-gather.10.cloned.1.call-done = bf16[8,4,128,128]{3,2,1,0:T(8,128)(2,1)} async-done(((bf16[1,4,128,128]{3,2,1,0:T(8,128)(2,1)}), bf16[8,4,128,128]{3,2,1,0:T(8,128)(2,1)}) %all-gather.10.cloned.1.call-update) | async-done | bytes 1048592 | tf_op jit(solution)/shard_map/all_gather | solution.py:24
  100.8 1.5 fusion.60
  102.3 10.9 %all_gather.44 = bf16[4,4,128,128]{3,2,1,0:T(8,128)(2,1)S(1)} all-gather(bf16[1,4,128,128]{3,2,1,0:T(8,128)(2,1)S(1)} %fusion.60), channel_id=1, replica_groups=mesh['seq_0'=4,'seq_1'=8,'seq_2'=2,'head'=4] {'seq_0'}, dimensions={0}, use_global_device_ids=true | all-gather | bytes 655360 | tf_op jit(solution)/shard_map/all_gather | solution.py:24
  113.2 1.4 add_subtract_fusion.1
  115.9 9.2 %all-gather.16.cloned.1.call-done = bf16[16,4,64,512]{3,2,1,0:T(8,128)(2,1)} async-done(((bf16[8,4,64,512]{3,2,1,0:T(8,128)(2,1)}), bf16[16,4,64,512]{3,2,1,0:T(8,128)(2,1)}) %all-gather.16.cloned.1.call-update) | async-done | bytes 4194320 | tf_op jit(solution)/shard_map/all_gather | solution.py:53
  125.1 4.7 %copy.65 = bf16[4,8,2,64,512]{4,3,2,1,0:T(8,128)(2,1)} copy(bf16[4,8,2,64,512]{4,3,0,1,2:T(8,128)(2,1)} %bitcast.168) | data formatting | bytes 8388608 | tf_op jit(solution)/shard_map/transpose | solution.py:56
  129.8 6.4 %copy.68 = bf16[512,4096]{1,0:T(8,128)(2,1)} copy(bf16[512,4096]{0,1:T(8,128)(2,1)} %bitcast.157) | data formatting | bytes 8388608 | tf_op jit(solution)/shard_map/dot_general | solution.py:124
  136.2 4.3 %multiply_reduce_fusion = (f32[256,4]{0,1:T(4,128)S(1)}, f32[1,256,4,128]{1,3,2,0:T(8,128)S(1)}) fusion(f32[1,256,4,128]{1,3,2,0:T(8,128)} %get-tuple-element.30, f32[256,4]{0,1:T(4,128)S(1)} %add_rsqrt_fusion, bf16[256,4096,1]{1,0,2:T(8,128)(2,1)} %reshape.325, bf16[4,128,4096]{2,1,0:T(8,128)(2,1)} %bitcast.169), kind=kOutput, calls=%fused_computation.40 | convolution fusion | flops 1074134016 | bytes 7348224 | tf_op jit(solution)/shard_map/dot_general | solution.py:124
  142.2 2.0 all-gather.4
  146.6 4.5 %convolution_bitcast_fusion = f32[4096,512]{0,1:T(8,128)} fusion(bf16[256,512]{0,1:T(8,128)(2,1)S(1)} %bitcast.172, bf16[256,4096]{1,0:T(8,128)(2,1)S(1)} %bitcast.163), kind=kOutput, calls=%fused_computation | convolution fusion | flops 1073741824 | bytes 10747904 | tf_op jit(solution)/shard_map/dot_general | solution.py:131
  151.1 9.1 %copy.90 = f32[4096,512]{1,0:T(8,128)} copy(f32[4096,512]{0,1:T(8,128)} %convolution_bitcast_fusion) | data formatting | bytes 16777216
  161.2 3.5 %convolution_convert_fusion = bf16[256,4096]{1,0:T(8,128)(2,1)S(1)} fusion(bf16[256,512]{0,1:T(8,128)(2,1)S(1)} %bitcast.173, bf16[4096,512]{1,0:T(8,128)(2,1)} %bitcast.158), kind=kOutput, calls=%fused_computation.1 | convolution fusion | flops 1074790400 | bytes 6553600 | tf_op jit(solution)/shard_map/dot_general | solution.py:121
  164.7 1.6 copy.125
  166.3 3.8 %all-to-all-start = ((bf16[4,256,1024]{2,1,0:T(8,128)(2,1)}), bf16[4,256,1024]{2,1,0:T(8,128)(2,1)S(1)}, u32[]{:S(2)}, u32[]{:S(2)}) async-start(bf16[4,256,1024]{2,1,0:T(8,128)(2,1)} %bitcast.162), calls=%async_computation | async-start | bytes 4194304 | tf_op jit(solution)/shard_map/all_to_all | solution.py:72
  170.1 2.0 copy.73
  172.1 2.0 copy.78
  174.1 1.4 fusion.1
  178.7 1.8 copy.81
  182.8 13.3 %all-to-all-done = bf16[4,256,1024]{2,1,0:T(8,128)(2,1)S(1)} async-done(((bf16[4,256,1024]{2,1,0:T(8,128)(2,1)}), bf16[4,256,1024]{2,1,0:T(8,128)(2,1)S(1)}, u32[]{:S(2)}, u32[]{:S(2)}) %all-to-all-start) | async-done | bytes 2097184 | tf_op jit(solution)/shard_map/all_to_all | solution.py:72
  196.0 1.3 reduce_sum.34
  197.4 1.6 fusion.59
  199.0 11.5 %all_gather.53 = bf16[4,4,128,128]{3,2,1,0:T(8,128)(2,1)S(1)} all-gather(bf16[1,4,128,128]{3,2,1,0:T(8,128)(2,1)S(1)} %fusion.59), channel_id=1, replica_groups=mesh['seq_0'=4,'seq_1'=8,'seq_2'=2,'head'=4] {'seq_0'}, dimensions={0}, use_global_device_ids=true | all-gather | bytes 655360 | tf_op jit(solution)/shard_map/all_gather | solution.py:24
  213.4 121.0 %reduce-scatter.4.cloned.1.call-done = f32[64,512]{1,0:T(8,128)} async-done(((f32[4096,512]{1,0:T(8,128)}), f32[64,512]{1,0:T(8,128)}) %reduce-scatter.4.cloned.1.call-update) | async-done | bytes 131088
  (84 shorter events, 21.4 us)
Async XLA Ops:
  7.2 14.8 %copy-start = (bf16[256,512]{1,0:T(8,128)(2,1)S(1)}, bf16[256,512]{1,0:T(8,128)(2,1)}, u32[]{:S(2)}) copy-start(bf16[256,512]{1,0:T(8,128)(2,1)} %param.7) | copy-start | bytes 786436
  7.2 54.5 %all-gather.14.cloned.1.call-start = ((), (), s32[]{:S(2)}) async-start(), calls=%async_computation.5 | async-start | bytes 2359296 | tf_op jit(solution)/shard_map/all_gather | solution.py:53
  19.8 81.0 %all-gather.10.cloned.1.call-start = ((), (), s32[]{:S(2)}) async-start(), calls=%async_computation.3 | async-start | bytes 1179648 | tf_op jit(solution)/shard_map/all_gather | solution.py:24
  21.8 46.9 %copy-start.4 = (bf16[32,4,8,128]{3,2,1,0:T(8,128)(2,1)}, bf16[32,4,8,128]{3,2,1,0:T(8,128)(2,1)S(1)}, u32[]{:S(2)}) copy-start(bf16[32,4,8,128]{3,2,1,0:T(8,128)(2,1)S(1)} %get-tuple-element.23) | copy-start | bytes 786436
  21.9 41.5 %copy-start.6 = (bf16[256,512]{0,1:T(8,128)(2,1)}, bf16[256,512]{0,1:T(8,128)(2,1)S(1)}, u32[]{:S(2)}) copy-start(bf16[256,512]{0,1:T(8,128)(2,1)S(1)} %copy.122) | copy-start | bytes 786436
  21.9 39.8 %copy-start.21 = (bf16[256,1024]{1,0:T(8,128)(2,1)S(1)}, bf16[256,1024]{1,0:T(8,128)(2,1)}, u32[]{:S(2)}) copy-start(bf16[256,1024]{1,0:T(8,128)(2,1)} %param.9) | copy-start | bytes 1572868
  28.8 34.6 %copy-start.12 = (bf16[8,128,128]{2,1,0:T(8,128)(2,1)}, bf16[8,128,128]{2,1,0:T(8,128)(2,1)S(1)}, u32[]{:S(2)}) copy-start(bf16[8,128,128]{2,1,0:T(8,128)(2,1)S(1)} %all-gather) | copy-start | bytes 786436
  29.5 95.6 %all-gather.16.cloned.1.call-start = ((), (), s32[]{:S(2)}) async-start(), calls=%async_computation.6 | async-start | bytes 6291456 | tf_op jit(solution)/shard_map/all_gather | solution.py:53
  63.4 4.1 %copy-start.22 = (bf16[256,512]{1,0:T(8,128)(2,1)S(1)}, bf16[256,512]{1,0:T(8,128)(2,1)}, u32[]{:S(2)}) copy-start(bf16[256,512]{1,0:T(8,128)(2,1)} %param.5) | copy-start | bytes 786436
  63.4 25.8 %all-to-all-start.1 = ((bf16[4,256,1024]{2,1,0:T(8,128)(2,1)}), bf16[4,256,1024]{2,1,0:T(8,128)(2,1)S(1)}, u32[]{:S(2)}, u32[]{:S(2)}) async-start(bf16[4,256,1024]{2,1,0:T(8,128)(2,1)} %broadcast_in_dim.12), calls=%async_computation.1 | async-start | bytes 4194304 | tf_op jit(solution)/shard_map/all_to_all | solution.py:36
  67.5 129.8 %all-gather.12.cloned.1.call-start = ((), (), s32[]{:S(2)}) async-start(), calls=%async_computation.4 | async-start | bytes 1179648 | tf_op jit(solution)/shard_map/all_gather | solution.py:24
  68.6 0.7 copy-start.7
  100.8 12.4 %copy-start.3 = (bf16[8,4,128,128]{3,2,1,0:T(8,128)(2,1)S(1)}, bf16[8,4,128,128]{3,2,1,0:T(8,128)(2,1)}, u32[]{:S(2)}) copy-start(bf16[8,4,128,128]{3,2,1,0:T(8,128)(2,1)} %all-gather.10.cloned.1.call-done) | copy-start | bytes 3145732
  100.8 13.9 %copy-start.17 = (f32[4,128,256]{2,1,0:T(8,128)S(1)}, f32[4,128,256]{2,1,0:T(8,128)}, u32[]{:S(2)}) copy-start(f32[4,128,256]{2,1,0:T(8,128)} %convolution_bitcast_fusion.8) | copy-start | bytes 1572868
  114.7 15.1 %copy-start.8 = (f32[4,128,128]{2,1,0:T(8,128)}, f32[4,128,128]{2,1,0:T(8,128)S(1)}, u32[]{:S(2)}) copy-start(f32[4,128,128]{2,1,0:T(8,128)S(1)} %add_subtract_fusion.1) | copy-start | bytes 786436
  136.2 4.3 %copy-start.15 = (f32[1,256,4,128]{1,3,2,0:T(8,128)S(1)}, f32[1,256,4,128]{1,3,2,0:T(8,128)}, u32[]{:S(2)}) copy-start(f32[1,256,4,128]{1,3,2,0:T(8,128)} %get-tuple-element.30) | copy-start | bytes 1572868
  144.2 0.7 copy-start.10
  145.6 188.8 %reduce-scatter.4.cloned.1.call-start = ((), (), s32[]{:S(2)}) async-start(), calls=%async_computation.7 | async-start | bytes 8519680
  145.7 1.0 copy-start.13
  160.2 0.9 copy-start.14
  166.3 29.8 %all-to-all-start = ((bf16[4,256,1024]{2,1,0:T(8,128)(2,1)}), bf16[4,256,1024]{2,1,0:T(8,128)(2,1)S(1)}, u32[]{:S(2)}, u32[]{:S(2)}) async-start(bf16[4,256,1024]{2,1,0:T(8,128)(2,1)} %bitcast.162), calls=%async_computation | async-start | bytes 4194304 | tf_op jit(solution)/shard_map/all_to_all | solution.py:72
  174.1 3.4 copy-start.9
  174.1 3.4 %copy-start.18 = (f32[256,512]{0,1:T(8,128)S(1)}, f32[256,512]{0,1:T(8,128)}, u32[]{:S(2)}) copy-start(f32[256,512]{0,1:T(8,128)} %copy.73) | copy-start | bytes 1572868
  175.5 0.8 copy-start.1
  182.7 27.7 %copy-start.11 = (bf16[8,128,128]{2,1,0:T(8,128)(2,1)S(1)}, bf16[8,128,128]{2,1,0:T(8,128)(2,1)}, u32[]{:S(2)}) copy-start(bf16[8,128,128]{2,1,0:T(8,128)(2,1)} %copy-done.10) | copy-start | bytes 786436
  182.7 27.7 %copy-start.20 = (f32[4,128,128]{2,1,0:T(8,128)S(1)}, f32[4,128,128]{2,1,0:T(8,128)}, u32[]{:S(2)}) copy-start(f32[4,128,128]{2,1,0:T(8,128)} %get-tuple-element.34) | copy-start | bytes 786436
  197.3 13.5 %copy-start.5 = (bf16[32,4,8,128]{3,2,1,0:T(8,128)(2,1)S(1)}, bf16[32,4,8,128]{3,2,1,0:T(8,128)(2,1)}, u32[]{:S(2)}) copy-start(bf16[32,4,8,128]{3,2,1,0:T(8,128)(2,1)} %copy-done.4) | copy-start | bytes 786436
  197.3 13.5 %copy-start.19 = (f32[1,256,4,128]{1,3,2,0:T(8,128)S(1)}, f32[1,256,4,128]{1,3,2,0:T(8,128)}, u32[]{:S(2)}) copy-start(f32[1,256,4,128]{1,3,2,0:T(8,128)} %convolution_bitcast_fusion.2) | copy-start | bytes 1572868
  197.4 13.1 %copy-start.2 = (bf16[8,4,128,128]{3,2,1,0:T(8,128)(2,1)S(1)}, bf16[8,4,128,128]{3,2,1,0:T(8,128)(2,1)}, u32[]{:S(2)}) copy-start(bf16[8,4,128,128]{3,2,1,0:T(8,128)(2,1)} %all-gather.12.cloned.1.call-done) | copy-start | bytes 3145732
  210.5 1.7 copy-start.16
Sparse Core Ops, SparseCore 0:
  19.9 41.7 all-gather.13
  64.0 36.7 all-gather.9
  102.6 22.4 all-gather.15
  145.7 34.2 all-gather.11
  184.0 150.3 reduce-scatter.3
where the time goes:
time: 348 us; the launch traced here: 343 us
  waiting for transfers between devices  198 us (57%)
  local copies, waits for them, and re-layouts  44.3 us (13%)
  blocking collectives  42.8 us (12%)
  matrix products  23.6 us (7%)
  between operations  14.1 us (4%)
  other arithmetic  11.4 us (3%)
  starting transfers between devices  8.09 us (2%)
    unnamed x6, waiting for transfers between devices  121 us
    all_gather x2, waiting for transfers between devices, gather_in_order(): parts = lax.all_gather(parts, axes[k])  41.3 us
    all_gather x4, blocking collectives, entering(): pieces = lax.all_gather(running.astype(jnp.bfloat16), axis)  30.3 us
    all_to_all x1, waiting for transfers between devices, from_everyone(): lax.all_to_all(jnp.broadcast_to(x[None], (peers, *x.shape)), axis, 0, 0,...  18.8 us
    unnamed x52, local copies, waits for them, and re-layouts  18 us
    all_to_all x1, waiting for transfers between devices, summed_on_arrival(): parts = lax.all_to_all(cut_along(x, dim, peers), axis, 0, 0, tiled=True)  13.3 us
    all_gather x1, blocking collectives, gather_in_order(): parts = lax.all_gather(parts, axes[k])  12.5 us
  transfers between devices with their start and end apart: 7, of which 6 were waited for; matrix products, arithmetic and copies ran while one was open for 16% of the time, Pallas kernels for 0%

commit v1 on v0

v1 whole, which is shorter than its diff:
```python
import functools

import jax
import jax.numpy as jnp
from jax import lax
from jax.experimental import pallas as pl
from jax.experimental.pallas import tpu as pltpu
from jax.sharding import Mesh
from jax.sharding import PartitionSpec as P

SEQ = ("seq_0", "seq_1", "seq_2")
NX, NZ, NC, NY = 4, 8, 2, 4
HD = 128
HEADS = 4
ROWS = 256
WIDTH = HEADS * HD
FEATS = 1024
EPS = 1e-06
WROWS = 64
WA = 16
COPIES = 176
MESH = pl.DeviceIdType.MESH
f32 = jnp.float32
bf16 = jnp.bfloat16


def nn(a, b):
    return lax.dot_general(a, b, (((1,), (0,)), ((), ())), preferred_element_type=f32)


def nt(a, b):
    return lax.dot_general(a, b, (((1,), (1,)), ((), ())), preferred_element_type=f32)


def tn(a, b):
    return lax.dot_general(a, b, (((0,), (0,)), ((), ())), preferred_element_type=f32)


def kernel(
    grad_scale,
    q_ref, k_ref, v_ref, w_ref, c_ref,
    lo_ref, qg_ref, kg_ref, vg_ref, dw_ref,
    qf, kf, scores, att, unit, inv, normed, datt, prior, kacc, vacc,
    state, own_b, sib_b, chip, zsend, zrecv, tsend, trecv, psend, pre,
    wall, call, csib, lsend, lrecv, ntown, ntsend, ntsib,
    xsend, xrecv, xsum, dsend, drecv, rsend, rrecv, zown, esend, erecv, mine, tsib_recv,
    ssem, rsem, lsem,
):
    x, z, c, y = (lax.axis_index(a) for a in (*SEQ, "head"))
    s = 1 - 2 * c

    def at(dx=0, dz=0, dc=0, dy=0):
        return (
            lax.rem(x + dx + NX, NX),
            lax.rem(z + dz + NZ, NZ),
            lax.rem(c + dc, NC),
            lax.rem(y + dy + NY, NY),
        )

    def zat(offset):
        return lax.rem(z + offset + 2 * NZ, NZ)

    peers = [at(dc=1)]
    peers += [at(dz=j) for j in range(1, NZ)]
    peers += [at(dx=j) for j in range(1, NX)]
    peers += [at(dy=j) for j in range(1, NY)]

    made = []

    def send(src, dst, device):
        n = len(made)
        copy = pltpu.make_async_remote_copy(
            src_ref=src, dst_ref=dst, send_sem=ssem.at[n], recv_sem=rsem.at[n],
            device_id=device, device_id_type=MESH,
        )
        copy.start()
        made.append(copy)
        return copy

    def cols(h):
        return pl.ds(h * HD, HD)

    def rows(h):
        return pl.ds(h * HD, HD)

    def phi(ref, h):
        a = ref[:, cols(h)].astype(f32)
        return jnp.where(a > 0, a + 1.0, jnp.exp(jnp.minimum(a, 0.0)))

    def slope(ref, h):
        a = ref[:, cols(h)].astype(f32)
        return jnp.where(a > 0, 1.0, jnp.exp(jnp.minimum(a, 0.0)))

    def causal():
        t = lax.broadcasted_iota(jnp.int32, (ROWS, ROWS), 0)
        u = lax.broadcasted_iota(jnp.int32, (ROWS, ROWS), 1)
        return u <= t

    half = 2 * HD
    piece = half // NZ
    lo_row = pl.multiple_of(half * c, half)

    def scan_begin(i):
        own_b[i] = state[...].astype(bf16)
        return send(own_b.at[i], sib_b.at[i], at(dc=1))

    def scan_chip(i, copy):
        copy.wait_recv()
        total = own_b[i, pl.ds(lo_row, half)].astype(f32) + sib_b[i, pl.ds(lo_row, half)].astype(f32)
        chip[...] = total
        zsend[i] = total.astype(bf16)
        out = []
        for j in range(1, NZ):
            d = zat(j)
            out.append(send(zsend.at[i, pl.ds(pl.multiple_of(d * piece, piece), piece)], zrecv.at[i, z], at(dz=j)))
        return out

    def scan_total(i, copies, reverse):
        for copy in copies:
            copy.wait_recv()
        zrecv[i, z] = zsend[i, pl.ds(pl.multiple_of(z * piece, piece), piece)]
        running = jnp.zeros((piece, HD), f32)
        inner = [None] * NZ
        for o in reversed(range(NZ)) if reverse else range(NZ):
            inner[o] = running
            running = running + zrecv[i, o].astype(f32)
        tsend[i] = running.astype(bf16)
        out = [send(tsend.at[i], trecv.at[i, x], at(dx=j)) for j in range(1, NX)]
        trecv[i, x] = tsend[i]
        return inner, out

    def scan_back(i, state_in, reverse):
        inner, copies = state_in
        for copy in copies:
            copy.wait_recv()
        outer = jnp.zeros((piece, HD), f32)
        for o in range(NX):
            passed = (o > x) if reverse else (o < x)
            outer = outer + jnp.where(passed, trecv[i, o].astype(f32), 0.0)
        for o in range(NZ):
            psend[i, o] = (inner[o] + outer).astype(bf16)
        place = pl.ds(pl.multiple_of(half * c + piece * z, piece), piece)
        out = [send(psend.at[i, zat(j)], pre.at[i, place], at(dz=j)) for j in range(1, NZ)]
        pre[i, place] = psend[i, z]
        return out

    def scan_share(i, copies):
        for copy in copies:
            copy.wait_recv()
        return send(pre.at[i, pl.ds(lo_row, half)], pre.at[i, pl.ds(lo_row, half)], at(dc=1))

    def scan_end(i, copy, reverse):
        copy.wait_recv()
        takes = (c == 0) if reverse else (c == 1)
        state[...] = pre[i].astype(f32) + jnp.where(takes, sib_b[i].astype(f32), 0.0)

    barrier = pltpu.get_barrier_semaphore()
    for peer in peers:
        pl.semaphore_signal(barrier, inc=1, device_id=peer, device_id_type=MESH)
    own_cot = pltpu.make_async_copy(c_ref, call.at[y], lsem.at[0])
    own_cot.start()
    wall[x, z, c] = w_ref[...]
    for h in range(HEADS):
        kh = phi(k_ref, h).astype(bf16)
        kf[:, cols(h)] = kh
        state[rows(h), :] = tn(kh, v_ref[:, cols(h)])
    pl.semaphore_wait(barrier, len(peers))

    scan = scan_begin(0)
    part_a = pl.ds(0, WA)
    part_b = pl.ds(WA, WROWS - WA)
    xa = [send(wall.at[x, z, c, part_a], wall.at[x, z, c, part_a], at(dx=j)) for j in range(1, NX)]

    def b_across(origin):
        return [
            send(wall.at[x, origin, c, part_b], wall.at[x, origin, c, part_b], at(dx=j)) for j in range(1, NX)
        ]

    def b_step(origin, way):
        return send(wall.at[x, origin, c, part_b], wall.at[x, origin, c, part_b], at(dz=way))

    def a_step(origin, way):
        return send(wall.at[:, origin, c, part_a], wall.at[:, origin, c, part_a], at(dz=way))

    bm = [b_step(z, s)]
    bo = [b_step(z, -s)]
    scan = scan_chip(0, scan)
    cot_y = [send(c_ref, call.at[y], at(dy=j)) for j in (2, 1, 3)]
    xb = {0: b_across(z)}
    cot_c = [send(c_ref, csib.at[y], at(dc=1))]

    am, ao = [], []

    def serve_b(i):
        bm[i].wait_recv()
        if i < 3:
            bm.append(b_step(zat(-s * (i + 1)), s))
        if i < 3:
            bo[i].wait_recv()
            if i < 2:
                bo.append(b_step(zat(s * (i + 1)), -s))
            xb[-i - 1] = b_across(zat(s * (i + 1)))
        xb[i + 1] = b_across(zat(-s * (i + 1)))

    def serve_a0():
        for copy in xa:
            copy.wait_recv()
        am.append(a_step(z, s))
        ao.append(a_step(z, -s))

    def serve_a(i):
        am[i].wait_recv()
        if i < 3:
            am.append(a_step(zat(-s * (i + 1)), s))
        if i < 3:
            ao[i].wait_recv()
            if i < 2:
                ao.append(a_step(zat(s * (i + 1)), -s))

    wsib = []

    def share_w(k):
        for copy in xb[k]:
            copy.wait_recv()
        origin = zat(-s * k)
        wsib.append(send(wall.at[:, origin, c], wall.at[:, origin, c], at(dc=1)))

    def intra(h):
        qh = phi(q_ref, h).astype(bf16)
        qf[:, cols(h)] = qh
        sc = jnp.where(causal(), nt(qh, kf[:, cols(h)]), 0.0).astype(bf16)
        scores[h] = sc
        att[:, cols(h)] = nn(sc, v_ref[:, cols(h)])

    intra(0)
    intra(1)
    serve_b(0)
    serve_a0()
    intra(2)
    intra(3)
    scan = scan_total(0, scan, False)
    serve_b(1)
    serve_a(0)
    scan = scan_back(0, scan, False)
    serve_b(2)
    serve_a(1)
    serve_b(3)
    share_w(0)
    scan = scan_share(0, scan)
    serve_a(2)
    scan_end(0, scan, False)

    for h in range(HEADS):
        st = state[rows(h), :].astype(bf16)
        a = att[:, cols(h)] + nn(qf[:, cols(h)], st)
        r = lax.rsqrt(jnp.mean(a * a, axis=-1, keepdims=True) + EPS)
        u = a * r
        unit[:, cols(h)] = u
        inv[:, cols(h)] = jnp.broadcast_to(r, (ROWS, HD))
        n = u.astype(bf16)
        normed[:, cols(h)] = n
        prior[rows(h), :] = st
        t = u.T.astype(bf16)
        ntsend[h // 2, pl.ds((h % 2) * HD, HD), :] = t
    nt_copy = send(ntsend.at[1 - c], ntsib, at(dc=1))
    ntown[...] = ntsend[c]

    for k in (1, -1, 2, -2):
        share_w(k)
    serve_a(3)
    for k in (3, -3, 4):
        share_w(k)
    for copy in wsib:
        copy.wait_recv()
    own_cot.wait()

    def weight(b):
        return wall[b].reshape(FEATS, WIDTH)

    lcopy = []
    for j in (2, 1, 3):
        d = lax.rem(y + j, NY)
        lsend[j] = nt(normed[...], weight(d)).astype(bf16)
        lcopy.append(send(lsend.at[j], lrecv.at[j - 1], at(dy=j)))
    lsend[0] = nt(normed[...], weight(y)).astype(bf16)

    for copy, j in zip(cot_y, (2, 1, 3)):
        copy.wait_recv()
        b = lax.rem(y - j + NY, NY)
        cot_c.append(send(call.at[b], csib.at[b], at(dc=1)))
    up = nn(call[0], weight(0))
    for b in range(1, NY):
        up = up + nn(call[b], weight(b))
    for h in range(HEADS):
        u = unit[:, cols(h)]
        d = up[:, h * HD : (h + 1) * HD]
        m = jnp.mean(d * u, axis=-1, keepdims=True)
        da = (inv[:, cols(h)] * (d - u * m)).astype(bf16)
        datt[:, cols(h)] = da
        state[rows(h), :] = tn(qf[:, cols(h)], da)
    scan = scan_begin(1)

    for copy in cot_c:
        copy.wait_recv()
    nt_copy.wait_recv()
    scan = scan_chip(1, scan)

    def x_part(b):
        return nn(ntown[pl.ds(HD, HD), :], call[b]) + nn(ntsib[pl.ds(HD, HD), :], csib[b])

    def z_part(d, b):
        at_d = pl.ds(pl.multiple_of(d * HD, HD), HD)
        return nn(ntown[pl.ds(0, HD), :], call[b, :, at_d]) + nn(ntsib[pl.ds(0, HD), :], csib[b, :, at_d])

    rm, ro = [], []

    def ring(i):
        far = zat(s * (4 - i))
        for b in range(NX):
            p = z_part(far, b)
            if i:
                p = p + rrecv[i - 1, b].astype(f32)
            rsend[i, b] = p.astype(bf16)
        rm.append(send(rsend.at[i], rrecv.at[i], at(dz=s)))
        if i < 3:
            far = zat(-s * (3 - i))
            for b in range(NX):
                p = z_part(far, b)
                if i:
                    p = p + rrecv[4 + i - 1, b].astype(f32)
                rsend[4 + i, b] = p.astype(bf16)
            ro.append(send(rsend.at[4 + i], rrecv.at[4 + i], at(dz=-s)))

    xcopy = []
    ring(0)
    for j in (2, 1, 3):
        d = lax.rem(x + j, NX)
        p = x_part(d).astype(bf16)
        for o in range(NZ):
            xsend[j - 1, o] = p[:, o * HD : (o + 1) * HD]
        xcopy.append(send(xsend.at[j - 1], xrecv.at[j - 1], at(dx=j)))
    p = x_part(x)
    for o in range(NZ):
        xsum[o] = p[:, o * HD : (o + 1) * HD]

    def grads(h):
        da = datt[:, cols(h)]
        vh = v_ref[:, cols(h)]
        ds = jnp.where(causal(), nt(da, vh), 0.0).astype(bf16)
        qg = nn(ds, kf[:, cols(h)]) + nt(da, prior[rows(h), :])
        qg_ref[:, cols(h)] = (qg * slope(q_ref, h)).astype(bf16)
        kacc[:, cols(h)] = tn(ds, qf[:, cols(h)])
        vacc[:, cols(h)] = tn(scores[h], da)

    rm[0].wait_recv()
    ro[0].wait_recv()
    ring(1)
    grads(0)
    scan = scan_total(1, scan, True)
    grads(1)
    rm[1].wait_recv()
    ro[1].wait_recv()
    ring(2)
    scan = scan_back(1, scan, True)
    grads(2)
    grads(3)
    rm[2].wait_recv()
    ro[2].wait_recv()
    ring(3)
    scan = scan_share(1, scan)
    for copy in xcopy:
        copy.wait_recv()
    dcopy = []
    for o in range(NZ):
        t = xsum[o]
        for j in range(NX - 1):
            t = t + xrecv[j, o].astype(f32)
        xsum[o] = t
        dsend[o] = t.astype(bf16)
    for j in range(1, NZ):
        dcopy.append(send(dsend.at[zat(j)], drecv.at[j - 1], at(dz=j)))
    scan_end(1, scan, True)
    for h in range(HEADS):
        st = state[rows(h), :].astype(bf16)
        kg = kacc[:, cols(h)] + nt(v_ref[:, cols(h)], st)
        kg_ref[:, cols(h)] = (kg * slope(k_ref, h)).astype(bf16)
        vg_ref[:, cols(h)] = (vacc[:, cols(h)] + nn(kf[:, cols(h)], st)).astype(bf16)

    rm[3].wait_recv()
    for b in range(NX):
        t = z_part(z, b) + rrecv[3, b].astype(f32) + rrecv[6, b].astype(f32)
        zown[b] = t
        esend[b] = t.astype(bf16)
    ecopy = [send(esend.at[lax.rem(x + j, NX)], erecv.at[j - 1], at(dx=j)) for j in range(1, NX)]

    total = lsend[0].astype(f32)
    for copy in lcopy:
        copy.wait_recv()
    for j in range(NY - 1):
        total = total + lrecv[j].astype(f32)
    lo_ref[...] = total.astype(bf16)

    for copy in ecopy:
        copy.wait_recv()
    t = zown[x]
    for j in range(NX - 1):
        t = t + erecv[j].astype(f32)
    mine[:, pl.ds(0, HD)] = t.T
    for copy in dcopy:
        copy.wait_recv()
    t = xsum[z]
    for j in range(NZ - 1):
        t = t + drecv[j].astype(f32)
    mine[:, pl.ds(HD, HD)] = t.T
    other = pl.multiple_of((1 - c) * WROWS, WROWS)
    last = send(mine.at[pl.ds(other, WROWS)], tsib_recv, at(dc=1))
    last.wait_recv()
    here = mine[pl.ds(pl.multiple_of(c * WROWS, WROWS), WROWS), :] * grad_scale
    there = tsib_recv[...] * grad_scale
    dw_ref[:, pl.ds(0, 2 * HD)] = jnp.where(c == 0, here, there)
    dw_ref[:, pl.ds(2 * HD, 2 * HD)] = jnp.where(c == 0, there, here)
    for copy in made:
        copy.wait_send()


def solution(mesh):
    split = Mesh(mesh.devices.reshape(NX, NZ, NC, NY), (*SEQ, "head"))
    placed = P(SEQ, "head")

    def shards(q, k, v, w, cot):
        shape = jax.ShapeDtypeStruct
        vm = pltpu.VMEM
        return pl.pallas_call(
            functools.partial(kernel, 16384.0**-0.5),
            out_shape=(
                shape((ROWS, FEATS), bf16),
                shape((ROWS, WIDTH), bf16),
                shape((ROWS, WIDTH), bf16),
                shape((ROWS, WIDTH), bf16),
                shape((WROWS, WIDTH), f32),
            ),
            in_specs=[pl.BlockSpec(memory_space=pltpu.VMEM)] * 5,
            out_specs=[pl.BlockSpec(memory_space=pltpu.VMEM)] * 5,
            scratch_shapes=[
                vm((ROWS, WIDTH), bf16),
                vm((ROWS, WIDTH), bf16),
                vm((HEADS, ROWS, ROWS), bf16),
                vm((ROWS, WIDTH), f32),
                vm((ROWS, WIDTH), f32),
                vm((ROWS, WIDTH), f32),
                vm((ROWS, WIDTH), bf16),
                vm((ROWS, WIDTH), bf16),
                vm((WIDTH, HD), bf16),
                vm((ROWS, WIDTH), f32),
                vm((ROWS, WIDTH), f32),
                vm((WIDTH, HD), f32),
                vm((2, WIDTH, HD), bf16),
                vm((2, WIDTH, HD), bf16),
                vm((2 * HD, HD), f32),
                vm((2, 2 * HD, HD), bf16),
                vm((2, NZ, 2 * HD // NZ, HD), bf16),
                vm((2, 2 * HD // NZ, HD), bf16),
                vm((2, NX, 2 * HD // NZ, HD), bf16),
                vm((2, NZ, 2 * HD // NZ, HD), bf16),
                vm((2, WIDTH, HD), bf16),
                vm((NX, NZ, NC, WROWS, WIDTH), bf16),
                vm((NY, ROWS, FEATS), bf16),
                vm((NY, ROWS, FEATS), bf16),
                vm((NY, ROWS, FEATS), bf16),
                vm((NY - 1, ROWS, FEATS), bf16),
                vm((2 * HD, ROWS), bf16),
                vm((2, 2 * HD, ROWS), bf16),
                vm((2 * HD, ROWS), bf16),
                vm((NX - 1, NZ, HD, HD), bf16),
                vm((NX - 1, NZ, HD, HD), bf16),
                vm((NZ, HD, HD), f32),
                vm((NZ, HD, HD), bf16),
                vm((NZ - 1, HD, HD), bf16),
                vm((7, NX, HD, HD), bf16),
                vm((7, NX, HD, HD), bf16),
                vm((NX, HD, HD), f32),
                vm((NX, HD, HD), bf16),
                vm((NX - 1, HD, HD), bf16),
                vm((HD, 2 * HD), f32),
                vm((WROWS, 2 * HD), f32),
                pltpu.SemaphoreType.DMA((COPIES,)),
                pltpu.SemaphoreType.DMA((COPIES,)),
                pltpu.SemaphoreType.DMA((1,)),
            ],
            compiler_params=pltpu.CompilerParams(
                collective_id=0, has_side_effects=True, vmem_limit_bytes=48 * 2**20
            ),
            name="layer_step",
        )(q, k, v, w, cot)

    return jax.shard_map(
        shards, mesh=split, in_specs=(placed,) * 5, out_specs=(placed,) * 5, check_vma=False
    )
```

time: 348 us -> 83.3 us (0.24); the launches traced: 343 us -> 83.1 us
  waiting for transfers between devices: 198 us -> 0 us
  Pallas kernels: 0 us -> 74.1 us
  blocking collectives: 42.8 us -> 0 us
  local copies, waits for them, and re-layouts: 44.3 us -> 8.28 us
  matrix products: 23.6 us -> 0 us
  between operations: 14.1 us -> 0.66 us
  other arithmetic: 11.4 us -> 0 us
  starting transfers between devices: 8.09 us -> 0 us
    unnamed x6 -> x0, waiting for transfers between devices: 121 us -> none
    pallas_call x0 -> x1, Pallas kernels: none -> 74.1 us  [shards(): pl.pallas_call(functools.partial(kernel, 16384.0 ** (-0.5)), out_shape=(s...]
    all_gather x4 -> x0, waiting for transfers between devices: 45.3 us -> none  [the longest x2 41.3 us: gather_in_order(): parts = lax.all_gather(parts, axes[k])]
    all_gather x5 -> x0, blocking collectives: 42.8 us -> none  [the longest x4 30.3 us: entering(): pieces = lax.all_gather(running.astype(jnp.bfloat16), axis)]
    all_to_all x2 -> x0, waiting for transfers between devices: 32 us -> none  [the longest x1 18.8 us: from_everyone(): lax.all_to_all(jnp.broadcast_to(x[None], (peers, *x.shape)), axis, 0, 0,...]
    dot_general x15 -> x0, matrix products: 23.6 us -> none  [the longest x1 4.51 us: shards(): lax.dot_general(dy_whole, normed, (((0,), (0,)), ((), ())), preferred_ele...]
    unnamed x52 -> x15, local copies, waits for them, and re-layouts: 18 us -> 8.28 us
    all_to_all x2 -> x0, starting transfers between devices: 7.92 us -> none  [the longest x1 4.13 us: from_everyone(): lax.all_to_all(jnp.broadcast_to(x[None], (peers, *x.shape)), axis, 0, 0,...]
  transfers between devices with their start and end apart: 7 -> 0, of which waited for: 6 -> 0; matrix products, arithmetic and copies ran while one was open for 16% -> 0% of each run, Pallas kernels for 0% -> 0%
where the time goes in v1:
time: 83.3 us; the launch traced here: 83.1 us
  Pallas kernels  74.1 us (89%)
  local copies, waits for them, and re-layouts  8.28 us (10%)
    pallas_call x1, Pallas kernels, shards(): pl.pallas_call(functools.partial(kernel, 16384.0 ** (-0.5)), out_shape=(s...  74.1 us
    unnamed x15, local copies, waits for them, and re-layouts  8.28 us

profile of v1, /device:TPU:1, one launch (start us, length us, event | category | flops | bytes accessed | tf_op | source)
XLA Modules:
  0.0 83.1 jit_solution(1605346864378531497)
XLA Ops:
  0.6 0.0 copy-start
  0.6 1.0 %copy-done = bf16[256,1024]{1,0:T(8,128)(2,1)S(1)} copy-done((bf16[256,1024]{1,0:T(8,128)(2,1)S(1)}, bf16[256,1024]{1,0:T(8,128)(2,1)}, u32[]{:S(2)}) %copy-start) | copy-done | bytes 524312
  1.7 0.0 copy-start.1
  1.7 0.9 %copy-done.1 = bf16[256,512]{1,0:T(8,128)(2,1)S(1)} copy-done((bf16[256,512]{1,0:T(8,128)(2,1)S(1)}, bf16[256,512]{1,0:T(8,128)(2,1)}, u32[]{:S(2)}) %copy-start.1) | copy-done | bytes 262168
  2.6 0.0 copy-start.2
  2.6 0.9 %copy-done.2 = bf16[256,512]{1,0:T(8,128)(2,1)S(1)} copy-done((bf16[256,512]{1,0:T(8,128)(2,1)S(1)}, bf16[256,512]{1,0:T(8,128)(2,1)}, u32[]{:S(2)}) %copy-start.2) | copy-done | bytes 262168
  3.6 0.0 copy-start.3
  3.6 0.9 %copy-done.3 = bf16[256,512]{1,0:T(8,128)(2,1)S(1)} copy-done((bf16[256,512]{1,0:T(8,128)(2,1)S(1)}, bf16[256,512]{1,0:T(8,128)(2,1)}, u32[]{:S(2)}) %copy-start.3) | copy-done | bytes 262168
  4.5 0.0 copy-start.4
  4.5 0.8 %copy-done.4 = bf16[64,512]{1,0:T(8,128)(2,1)S(1)} copy-done((bf16[64,512]{1,0:T(8,128)(2,1)S(1)}, bf16[64,512]{1,0:T(8,128)(2,1)}, u32[]{:S(2)}) %copy-start.4) | copy-done | bytes 65560
  5.4 74.1 %layer_step.1 = (bf16[256,1024]{1,0:T(8,128)(2,1)S(1)}, bf16[256,512]{1,0:T(8,128)(2,1)S(1)}, bf16[256,512]{1,0:T(8,128)(2,1)S(1)}, bf16[256,512]{1,0:T(8,128)(2,1)S(1)}, f32[64,512]{1,0:T(8,128)S(1)}) custom-call(bf16[256,512]{1,0:T(8,128)(2,1)S(1)} %copy-done.1, bf16[256,512]{1,0:T(8,128)(2,1)S(1)} %copy-done.2, bf16[256,512]{1,0:T(8,128)(2,1)S(1)} %copy-done.3, ...), custom_call_target="tpu_custom_call" | custom-call | tf_op jit(solution)/shard_map/layer_step/pallas_call | solution.py:433
  79.5 0.8 copy.15
  80.3 0.7 copy.16
  81.0 0.7 copy.17
  81.7 0.7 copy.18
  82.4 0.7 copy.19
Async XLA Ops:
  0.6 1.0 %copy-start = (bf16[256,1024]{1,0:T(8,128)(2,1)S(1)}, bf16[256,1024]{1,0:T(8,128)(2,1)}, u32[]{:S(2)}) copy-start(bf16[256,1024]{1,0:T(8,128)(2,1)} %c_ref.1) | copy-start | bytes 1572868
  1.7 0.9 %copy-start.1 = (bf16[256,512]{1,0:T(8,128)(2,1)S(1)}, bf16[256,512]{1,0:T(8,128)(2,1)}, u32[]{:S(2)}) copy-start(bf16[256,512]{1,0:T(8,128)(2,1)} %q_ref.1) | copy-start | bytes 786436
  2.6 0.9 %copy-start.2 = (bf16[256,512]{1,0:T(8,128)(2,1)S(1)}, bf16[256,512]{1,0:T(8,128)(2,1)}, u32[]{:S(2)}) copy-start(bf16[256,512]{1,0:T(8,128)(2,1)} %k_ref.1) | copy-start | bytes 786436
  3.6 0.9 %copy-start.3 = (bf16[256,512]{1,0:T(8,128)(2,1)S(1)}, bf16[256,512]{1,0:T(8,128)(2,1)}, u32[]{:S(2)}) copy-start(bf16[256,512]{1,0:T(8,128)(2,1)} %v_ref.1) | copy-start | bytes 786436
  4.5 0.8 %copy-start.4 = (bf16[64,512]{1,0:T(8,128)(2,1)S(1)}, bf16[64,512]{1,0:T(8,128)(2,1)}, u32[]{:S(2)}) copy-start(bf16[64,512]{1,0:T(8,128)(2,1)} %w_ref.1) | copy-start | bytes 196612

commit v2 on v1

v2 whole, which is shorter than its diff:
```python
import functools

import jax
import jax.numpy as jnp
from jax import lax
from jax.experimental import pallas as pl
from jax.experimental.pallas import tpu as pltpu
from jax.sharding import Mesh
from jax.sharding import PartitionSpec as P

SEQ = ("seq_0", "seq_1", "seq_2")
NX, NZ, NC, NY = 4, 8, 2, 4
HD = 128
HEADS = 4
ROWS = 256
WIDTH = HEADS * HD
FEATS = 1024
EPS = 1e-06
WROWS = 64
WA = 16
ARRIVALS = 84
DEPARTURES = 20
MESH = pl.DeviceIdType.MESH
f32 = jnp.float32
bf16 = jnp.bfloat16


def nn(a, b):
    return lax.dot_general(a, b, (((1,), (0,)), ((), ())), preferred_element_type=f32)


def nt(a, b):
    return lax.dot_general(a, b, (((1,), (1,)), ((), ())), preferred_element_type=f32)


def tn(a, b):
    return lax.dot_general(a, b, (((0,), (0,)), ((), ())), preferred_element_type=f32)


def kernel(
    grad_scale,
    q_hbm, k_hbm, v_hbm, w_hbm, c_hbm,
    lo_ref, qg_ref, kg_ref, vg_ref, dw_ref,
    q_ref, k_ref, v_ref, qf, kf, scores, att, unit, inv, normed, datt, prior, kacc, vacc,
    state, own_b, sib_b, zsend, zrecv, tsend, trecv, psend, pre,
    wall, call, csib, lout, lsend, lrecv, lfar, ntown, ntsend, ntsib,
    pz, xsend, xrecv, xsum, dsend, drecv, rsend, rrecv, zown, esend, erecv, mine, tsib_recv,
    ssem, rsem, lsem,
):
    x, z, c, y = (lax.axis_index(a) for a in (*SEQ, "head"))
    s = 1 - 2 * c

    def at(dx=0, dz=0, dc=0, dy=0):
        return (
            lax.rem(x + dx + NX, NX),
            lax.rem(z + dz + NZ, NZ),
            lax.rem(c + dc, NC),
            lax.rem(y + dy + NY, NY),
        )

    def zat(offset):
        return lax.rem(z + offset + 2 * NZ, NZ)

    peers = [at(dc=1)]
    peers += [at(dz=j) for j in range(1, NZ)]
    peers += [at(dx=j) for j in range(1, NX)]
    peers += [at(dy=j) for j in range(1, NY)]

    kinds = {}
    arrivals = []

    def arrival():
        arrivals.append(None)
        return rsem.at[len(arrivals) - 1]

    def send(src, dst, device, kind, landed=None):
        copy = pltpu.make_async_remote_copy(
            src_ref=src, dst_ref=dst, send_sem=ssem.at[kinds.setdefault(kind, len(kinds))],
            recv_sem=arrival() if landed is None else landed,
            device_id=device, device_id_type=MESH,
        )
        copy.start()
        return copy

    def await_all(ref, sem):
        pltpu.make_async_copy(ref, ref, sem).wait()

    def sent(kind, ref):
        await_all(ref, ssem.at[kinds.pop(kind)])

    def cols(h):
        return pl.ds(h * HD, HD)

    def rows(h):
        return pl.ds(h * HD, HD)

    def phi(ref, h):
        a = ref[:, cols(h)].astype(f32)
        return jnp.where(a > 0, a + 1.0, jnp.exp(jnp.minimum(a, 0.0)))

    def slope(ref, h):
        a = ref[:, cols(h)].astype(f32)
        return jnp.where(a > 0, 1.0, jnp.exp(jnp.minimum(a, 0.0)))

    def causal():
        t = lax.broadcasted_iota(jnp.int32, (ROWS, ROWS), 0)
        u = lax.broadcasted_iota(jnp.int32, (ROWS, ROWS), 1)
        return u <= t

    half = 2 * HD
    piece = half // NZ
    lo_row = pl.multiple_of(half * c, half)

    def scan_begin(i):
        own_b[i] = state[...].astype(bf16)
        return send(own_b.at[i], sib_b.at[i], at(dc=1), "own")

    def scan_chip(i, copy):
        copy.wait_recv()
        total = own_b[i, pl.ds(lo_row, half)].astype(f32) + sib_b[i, pl.ds(lo_row, half)].astype(f32)
        zsend[i] = total.astype(bf16)
        landed = arrival()
        for j in range(1, NZ):
            rows_of = pl.ds(pl.multiple_of(zat(j) * piece, piece), piece)
            send(zsend.at[i, rows_of], zrecv.at[i, z], at(dz=j), "chip", landed)
        return landed

    def scan_total(i, landed, reverse):
        await_all(zrecv.at[i, pl.ds(0, NZ - 1)], landed)
        zrecv[i, z] = zsend[i, pl.ds(pl.multiple_of(z * piece, piece), piece)]
        running = jnp.zeros((piece, HD), f32)
        inner = [None] * NZ
        for o in reversed(range(NZ)) if reverse else range(NZ):
            inner[o] = running
            running = running + zrecv[i, o].astype(f32)
        tsend[i] = running.astype(bf16)
        landed = arrival()
        for j in range(1, NX):
            send(tsend.at[i], trecv.at[i, x], at(dx=j), "total", landed)
        return inner, landed

    def scan_back(i, state_in, reverse):
        inner, landed = state_in
        await_all(trecv.at[i, pl.ds(0, NX - 1)], landed)
        trecv[i, x] = tsend[i]
        outer = jnp.zeros((piece, HD), f32)
        for o in range(NX):
            passed = (o > x) if reverse else (o < x)
            outer = outer + jnp.where(passed, trecv[i, o].astype(f32), 0.0)
        for o in range(NZ):
            psend[i, o] = (inner[o] + outer).astype(bf16)
        place = pl.ds(pl.multiple_of(half * c + piece * z, piece), piece)
        landed = arrival()
        for j in range(1, NZ):
            send(psend.at[i, zat(j)], pre.at[i, place], at(dz=j), "back", landed)
        pre[i, place] = psend[i, z]
        return landed

    def scan_share(i, landed):
        await_all(psend.at[i, pl.ds(0, NZ - 1)], landed)
        return send(pre.at[i, pl.ds(lo_row, half)], pre.at[i, pl.ds(lo_row, half)], at(dc=1), "share")

    def scan_end(i, copy, reverse):
        copy.wait_recv()
        takes = (c == 0) if reverse else (c == 1)
        state[...] = pre[i].astype(f32) + jnp.where(takes, sib_b[i].astype(f32), 0.0)

    barrier = pltpu.get_barrier_semaphore()
    for peer in peers:
        pl.semaphore_signal(barrier, inc=1, device_id=peer, device_id_type=MESH)
    def load(i, src, dst):
        copy = pltpu.make_async_copy(src, dst, lsem.at[i])
        copy.start()
        return copy

    k_in = load(0, k_hbm, k_ref)
    v_in = load(1, v_hbm, v_ref)
    w_in = load(2, w_hbm, wall.at[x, z, c])
    c_in = load(3, c_hbm, call.at[y])
    q_in = load(4, q_hbm, q_ref)
    k_in.wait()
    v_in.wait()
    for h in range(HEADS):
        kh = phi(k_ref, h).astype(bf16)
        kf[:, cols(h)] = kh
        state[rows(h), :] = tn(kh, v_ref[:, cols(h)])
    for copy in (w_in, c_in, q_in):
        copy.wait()
    pl.semaphore_wait(barrier, len(peers))

    scan = scan_begin(0)
    part_a = pl.ds(0, WA)
    part_b = pl.ds(WA, WROWS - WA)
    xa = arrival()
    for j in range(1, NX):
        send(wall.at[x, z, c, part_a], wall.at[x, z, c, part_a], at(dx=j), "xa", xa)
    left, right = pl.ds(0, 2 * HD), pl.ds(2 * HD, 2 * HD)
    left_x, right_x = lax.rem(x + NX - 1, NX), lax.rem(x + 1, NX)

    def place(k):
        return zat(-s * k)

    def b_across(k):
        block = wall.at[x, place(k), c, part_b]
        return send(block, block, at(dx=1), "bx"), send(block, block, at(dx=-1), "bx")

    def b_relay(k):
        up_copy, down_copy = xb[k]
        landed = arrival()
        up_copy.wait_recv()
        block = wall.at[left_x, place(k), c, part_b, left]
        send(block, block, at(dx=1), "br", landed)
        down_copy.wait_recv()
        block = wall.at[right_x, place(k), c, part_b, right]
        send(block, block, at(dx=-1), "br", landed)
        xr[k] = landed

    def b_step(origin, way):
        block = wall.at[x, origin, c, part_b]
        return send(block, block, at(dz=way), "b")

    def a_step(origin, way):
        group = wall.at[:, origin, c, part_a]
        return send(group, group, at(dz=way), "a")

    bm = [b_step(z, s)]
    bo = [b_step(z, -s)]
    top, bottom = pl.ds(0, ROWS // 2), pl.ds(ROWS // 2, ROWS // 2)
    up_y, down_y = lax.rem(y + 1, NY), lax.rem(y + NY - 1, NY)
    far_y = lax.rem(y + 2, NY)

    def cot(b, part, way):
        return send(call.at[b, part], call.at[b, part], at(dy=way), "cot")

    p_top = cot(y, top, 1)
    m_bottom = cot(y, bottom, -1)
    p_bottom = cot(y, bottom, 1)
    m_top = cot(y, top, -1)
    xb, xr = {0: b_across(0)}, {}
    scan = scan_chip(0, scan)

    def cot_share(b):
        return send(call.at[b], csib.at[b], at(dc=1), "cot2")

    cot_c = {0: cot_share(y)}
    am, ao = [], []

    def serve_b(i):
        bm[i].wait_recv()
        if i < 3:
            bm.append(b_step(place(i + 1), s))
            bo[i].wait_recv()
            if i < 2:
                bo.append(b_step(place(-i - 1), -s))
            xb[-i - 1] = b_across(-i - 1)
        xb[i + 1] = b_across(i + 1)

    def serve_a0():
        await_all(wall.at[pl.ds(0, NX - 1), 0, 0, part_a], xa)
        am.append(a_step(z, s))
        ao.append(a_step(z, -s))

    def serve_a(i):
        am[i].wait_recv()
        if i < 3:
            am.append(a_step(place(i + 1), s))
            ao[i].wait_recv()
            if i < 2:
                ao.append(a_step(place(-i - 1), -s))

    wsib = arrival()

    def share_w(k):
        await_all(wall.at[0, 0, 0, part_b], xr[k])
        group = wall.at[:, place(k), c]
        send(group, group, at(dc=1), "wshare", wsib)

    def intra(h):
        qh = phi(q_ref, h).astype(bf16)
        qf[:, cols(h)] = qh
        sc = jnp.where(causal(), nt(qh, kf[:, cols(h)]), 0.0).astype(bf16)
        scores[h] = sc
        att[:, cols(h)] = nn(sc, v_ref[:, cols(h)])

    for h in range(HEADS):
        intra(h)
    serve_b(0)
    serve_a0()
    b_relay(0)
    scan = scan_total(0, scan, False)
    serve_b(1)
    b_relay(1)
    b_relay(-1)
    serve_a(0)
    p_top.wait_recv()
    f_top = cot(down_y, top, 1)
    m_bottom.wait_recv()
    f_bottom = cot(up_y, bottom, -1)
    scan = scan_back(0, scan, False)
    serve_b(2)
    b_relay(2)
    b_relay(-2)
    serve_a(1)
    share_w(0)
    serve_b(3)
    b_relay(3)
    b_relay(-3)
    scan = scan_share(0, scan)
    serve_a(2)
    share_w(1)
    share_w(-1)
    scan_end(0, scan, False)

    for h in range(HEADS):
        st = state[rows(h), :].astype(bf16)
        a = att[:, cols(h)] + nn(qf[:, cols(h)], st)
        r = lax.rsqrt(jnp.mean(a * a, axis=-1, keepdims=True) + EPS)
        u = a * r
        unit[:, cols(h)] = u
        inv[:, cols(h)] = jnp.broadcast_to(r, (ROWS, HD))
        n = u.astype(bf16)
        normed[:, cols(h)] = n
        prior[rows(h), :] = st
        t = u.T.astype(bf16)
        ntsend[h // 2, pl.ds((h % 2) * HD, HD), :] = t
    nt_copy = send(ntsend.at[1 - c], ntsib, at(dc=1), "nt")
    ntown[...] = ntsend[c]
    m_top.wait_recv()
    cot_c[1] = cot_share(up_y)
    b_relay(4)
    share_w(2)
    share_w(-2)
    serve_a(3)
    p_bottom.wait_recv()
    cot_c[3] = cot_share(down_y)

    half_rows = HD // 2

    def products(j):
        b = lax.rem(y + j, NY)
        cot_c[j].wait_recv()
        p = nn(ntown[...], call[b]) + nn(ntsib[...], csib[b])
        for o in range(NZ):
            lanes = slice(o * HD, (o + 1) * HD)
            pz[j, o] = p[:HD, lanes]
            xsend[0, j, o] = p[HD : HD + half_rows, lanes].astype(bf16)
            xsend[1, j, o] = p[HD + half_rows :, lanes].astype(bf16)

    rm, ro = ([], []), ([], [])
    groups = ((0, 1), (3, 2))

    def ring(g, i):
        if i:
            rm[g][i - 1].wait_recv()
        far = zat(s * (4 - i))
        for n, j in enumerate(groups[g]):
            p = pz[j, far]
            if i:
                p = p + rrecv[g, i - 1, n].astype(f32)
            rsend[g, i, n] = p.astype(bf16)
        rm[g].append(send(rsend.at[g, i], rrecv.at[g, i], at(dz=s), "ring"))
        if i < 3:
            if i:
                ro[g][i - 1].wait_recv()
            far = zat(-s * (3 - i))
            for n, j in enumerate(groups[g]):
                p = pz[j, far]
                if i:
                    p = p + rrecv[g, 4 + i - 1, n].astype(f32)
                rsend[g, 4 + i, n] = p.astype(bf16)
            ro[g].append(send(rsend.at[g, 4 + i], rrecv.at[g, 4 + i], at(dz=-s), "ring"))

    def ring_end(g):
        rm[g][3].wait_recv()
        ro[g][2].wait_recv()
        for n, j in enumerate(groups[g]):
            t = pz[j, z] + rrecv[g, 3, n].astype(f32) + rrecv[g, 6, n].astype(f32)
            zown[j] = t
            esend[j] = t.astype(bf16)

    def place_of(dx):
        return lax.rem(x + dx - y + 2 * NX, NX)

    def x_send(g):
        landed = arrival()
        for j in (2, 1, 3):
            send(xsend.at[g, place_of(j)], xrecv.at[g, j - 1], at(dx=j), "x", landed)
        return landed

    def x_sum(g, landed):
        await_all(xrecv.at[g], landed)
        for o in range(NZ):
            t = xsend[g, place_of(0), o].astype(f32)
            for j in range(NX - 1):
                t = t + xrecv[g, j, o].astype(f32)
            xsum[g, o] = t
            dsend[g, o] = t.astype(bf16)
        landed = arrival()
        for j in range(1, NZ):
            send(dsend.at[g, zat(j)], drecv.at[g, j - 1], at(dz=j), "d", landed)
        return landed

    nt_copy.wait_recv()
    products(0)
    products(1)
    ring(0, 0)
    products(3)
    share_w(3)
    share_w(-3)
    share_w(4)

    f_top.wait_recv()
    f_bottom.wait_recv()
    cot_c[2] = cot_share(far_y)
    products(2)
    ring(1, 0)
    x0 = x_send(0)
    x1 = x_send(1)

    def weight(b):
        return wall[b].reshape(FEATS, WIDTH)

    await_all(wall.at[pl.ds(0, 2)], wsib)
    lsend[2] = nt(normed[...], weight(far_y)).astype(bf16)
    l_far = [
        send(lsend.at[2, top], lfar.at[0], at(dy=1), "layer"),
        send(lsend.at[2, bottom], lfar.at[1], at(dy=-1), "layer"),
    ]
    up = nn(call[0], weight(0))
    for b in range(1, NY):
        up = up + nn(call[b], weight(b))
    for h in range(HEADS):
        u = unit[:, cols(h)]
        d = up[:, h * HD : (h + 1) * HD]
        m = jnp.mean(d * u, axis=-1, keepdims=True)
        da = (inv[:, cols(h)] * (d - u * m)).astype(bf16)
        datt[:, cols(h)] = da
        state[rows(h), :] = tn(qf[:, cols(h)], da)
    scan = scan_begin(1)
    near = arrival()
    lout[0] = nt(normed[...], weight(up_y))
    lsend[0, bottom] = lout[0, bottom].astype(bf16)
    send(lsend.at[0, bottom], lrecv.at[0, bottom], at(dy=1), "layer", near)
    lout[1] = nt(normed[...], weight(down_y))
    lsend[1, top] = lout[1, top].astype(bf16)
    send(lsend.at[1, top], lrecv.at[1, top], at(dy=-1), "layer", near)

    def layer_pass():
        l_far[0].wait_recv()
        lsend[0, top] = (lout[0, top] + lfar[0].astype(f32)).astype(bf16)
        send(lsend.at[0, top], lrecv.at[0, top], at(dy=1), "layer", near)
        l_far[1].wait_recv()
        lsend[1, bottom] = (lout[1, bottom] + lfar[1].astype(f32)).astype(bf16)
        send(lsend.at[1, bottom], lrecv.at[1, bottom], at(dy=-1), "layer", near)
        lout[2] = nt(normed[...], weight(y))

    ring(0, 1)
    scan = scan_chip(1, scan)

    def grads(h):
        da = datt[:, cols(h)]
        vh = v_ref[:, cols(h)]
        ds = jnp.where(causal(), nt(da, vh), 0.0).astype(bf16)
        qg = nn(ds, kf[:, cols(h)]) + nt(da, prior[rows(h), :])
        qg_ref[:, cols(h)] = (qg * slope(q_ref, h)).astype(bf16)
        kacc[:, cols(h)] = tn(ds, qf[:, cols(h)])
        vacc[:, cols(h)] = tn(scores[h], da)

    ring(1, 1)
    ring(0, 2)
    for h in range(HEADS):
        grads(h)
    scan = scan_total(1, scan, True)
    ring(1, 2)
    layer_pass()
    ring(0, 3)
    d0 = x_sum(0, x0)
    ring(1, 3)
    scan = scan_back(1, scan, True)
    ring_end(0)
    d1 = x_sum(1, x1)
    ring_end(1)
    landed_e = arrival()
    for j in range(1, NX):
        send(esend.at[place_of(j)], erecv.at[j - 1], at(dx=j), "e", landed_e)
    scan = scan_share(1, scan)
    scan_end(1, scan, True)
    for h in range(HEADS):
        st = state[rows(h), :].astype(bf16)
        kg = kacc[:, cols(h)] + nt(v_ref[:, cols(h)], st)
        kg_ref[:, cols(h)] = (kg * slope(k_ref, h)).astype(bf16)
        vg_ref[:, cols(h)] = (vacc[:, cols(h)] + nn(kf[:, cols(h)], st)).astype(bf16)

    await_all(lrecv, near)
    lo_ref[...] = (lout[2] + lrecv[0].astype(f32) + lrecv[1].astype(f32)).astype(bf16)

    await_all(erecv, landed_e)
    t = zown[place_of(0)]
    for j in range(NX - 1):
        t = t + erecv[j].astype(f32)
    mine[:, pl.ds(0, HD)] = t.T
    for g, landed in enumerate((d0, d1)):
        await_all(drecv.at[g], landed)
        t = xsum[g, z]
        for j in range(NZ - 1):
            t = t + drecv[g, j].astype(f32)
        xsum[g, z] = t
    mine[:, pl.ds(HD, HD)] = jnp.concatenate([xsum[0, z], xsum[1, z]], axis=0).T
    other = pl.multiple_of((1 - c) * WROWS, WROWS)
    last = send(mine.at[pl.ds(other, WROWS)], tsib_recv, at(dc=1), "last")
    last.wait_recv()
    here = mine[pl.ds(pl.multiple_of(c * WROWS, WROWS), WROWS), :] * grad_scale
    there = tsib_recv[...] * grad_scale
    dw_ref[:, pl.ds(0, 2 * HD)] = jnp.where(c == 0, here, there)
    dw_ref[:, pl.ds(2 * HD, 2 * HD)] = jnp.where(c == 0, there, here)
    sent("own", own_b)
    sent("chip", zrecv.at[:, pl.ds(0, NZ - 1)])
    sent("total", trecv.at[:, pl.ds(0, NX - 1)])
    sent("back", psend.at[:, pl.ds(0, NZ - 1)])
    sent("share", pre.at[:, pl.ds(0, half)])
    sent("xa", wall.at[pl.ds(0, NX - 1), 0, 0, part_a])
    sent("b", wall.at[0, pl.ds(0, NZ - 1), 0, part_b])
    sent("bx", wall.at[pl.ds(0, 2), :, 0, part_b])
    sent("br", wall.at[0, :, 0, part_b])
    sent("a", wall.at[:, pl.ds(0, NZ - 1), 0, part_a])
    sent("wshare", wall.at[pl.ds(0, 2)])
    sent("cot", call.at[pl.ds(0, 3)])
    sent("cot2", call)
    sent("nt", ntsib)
    sent("layer", lsend)
    sent("ring", rsend)
    sent("x", xrecv)
    sent("d", drecv)
    sent("e", erecv)
    sent("last", tsib_recv)
    assert not kinds and len(arrivals) == ARRIVALS


def write_out(*refs):
    sem = refs[-1]
    copies = [pltpu.make_async_copy(refs[i], refs[5 + i], sem.at[i]) for i in range(5)]
    for copy in copies:
        copy.start()
    for copy in copies:
        copy.wait()


def solution(mesh):
    split = Mesh(mesh.devices.reshape(NX, NZ, NC, NY), (*SEQ, "head"))
    placed = P(SEQ, "head")

    def shards(q, k, v, w, cot):
        shape = jax.ShapeDtypeStruct
        vm = pltpu.VMEM
        found = pl.pallas_call(
            functools.partial(kernel, 16384.0**-0.5),
            out_shape=(
                shape((ROWS, FEATS), bf16),
                shape((ROWS, WIDTH), bf16),
                shape((ROWS, WIDTH), bf16),
                shape((ROWS, WIDTH), bf16),
                shape((WROWS, WIDTH), f32),
            ),
            in_specs=[pl.BlockSpec(memory_space=pltpu.HBM)] * 5,
            out_specs=[pl.BlockSpec(memory_space=pltpu.VMEM)] * 5,
            scratch_shapes=[
                vm((ROWS, WIDTH), bf16),
                vm((ROWS, WIDTH), bf16),
                vm((ROWS, WIDTH), bf16),
                vm((ROWS, WIDTH), bf16),
                vm((ROWS, WIDTH), bf16),
                vm((HEADS, ROWS, ROWS), bf16),
                vm((ROWS, WIDTH), f32),
                vm((ROWS, WIDTH), f32),
                vm((ROWS, WIDTH), f32),
                vm((ROWS, WIDTH), bf16),
                vm((ROWS, WIDTH), bf16),
                vm((WIDTH, HD), bf16),
                vm((ROWS, WIDTH), f32),
                vm((ROWS, WIDTH), f32),
                vm((WIDTH, HD), f32),
                vm((2, WIDTH, HD), bf16),
                vm((2, WIDTH, HD), bf16),
                vm((2, 2 * HD, HD), bf16),
                vm((2, NZ, 2 * HD // NZ, HD), bf16),
                vm((2, 2 * HD // NZ, HD), bf16),
                vm((2, NX, 2 * HD // NZ, HD), bf16),
                vm((2, NZ, 2 * HD // NZ, HD), bf16),
                vm((2, WIDTH, HD), bf16),
                vm((NX, NZ, NC, WROWS, WIDTH), bf16),
                vm((NY, ROWS, FEATS), bf16),
                vm((NY, ROWS, FEATS), bf16),
                vm((3, ROWS, FEATS), f32),
                vm((3, ROWS, FEATS), bf16),
                vm((2, ROWS, FEATS), bf16),
                vm((2, ROWS // 2, FEATS), bf16),
                vm((2 * HD, ROWS), bf16),
                vm((2, 2 * HD, ROWS), bf16),
                vm((2 * HD, ROWS), bf16),
                vm((NX, NZ, HD, HD), f32),
                vm((2, NX, NZ, HD // 2, HD), bf16),
                vm((2, NX - 1, NZ, HD // 2, HD), bf16),
                vm((2, NZ, HD // 2, HD), f32),
                vm((2, NZ, HD // 2, HD), bf16),
                vm((2, NZ - 1, HD // 2, HD), bf16),
                vm((2, 7, 2, HD, HD), bf16),
                vm((2, 7, 2, HD, HD), bf16),
                vm((NX, HD, HD), f32),
                vm((NX, HD, HD), bf16),
                vm((NX - 1, HD, HD), bf16),
                vm((HD, 2 * HD), f32),
                vm((WROWS, 2 * HD), f32),
                pltpu.SemaphoreType.DMA((DEPARTURES,)),
                pltpu.SemaphoreType.DMA((ARRIVALS,)),
                pltpu.SemaphoreType.DMA((5,)),
            ],
            compiler_params=pltpu.CompilerParams(
                collective_id=0, has_side_effects=True, vmem_limit_bytes=56 * 2**20
            ),
            name="layer_step",
        )(q, k, v, w, cot)
        return pl.pallas_call(
            write_out,
            out_shape=[shape(a.shape, a.dtype) for a in found],
            in_specs=[pl.BlockSpec(memory_space=pltpu.VMEM)] * 5,
            out_specs=[pl.BlockSpec(memory_space=pltpu.HBM)] * 5,
            scratch_shapes=[pltpu.SemaphoreType.DMA((5,))],
            name="write_out",
        )(*found)

    return jax.shard_map(
        shards, mesh=split, in_specs=(placed,) * 5, out_specs=(placed,) * 5, check_vma=False
    )
```

time: 83.3 us -> 65.2 us (0.78)
  Pallas kernels: 74.1 us -> 64.4 us
  local copies, waits for them, and re-layouts: 8.28 us -> 0 us
    pallas_call x1, Pallas kernels: 74.1 us -> 62 us  [shards(): pl.pallas_call(functools.partial(kernel, 16384.0 ** (-0.5)), out_shape=(s...]
    unnamed x15 -> x0, local copies, waits for them, and re-layouts: 8.28 us -> none
    pallas_call x0 -> x1, Pallas kernels: none -> 2.43 us  [shards(): pl.pallas_call(write_out, out_shape=[shape(a.shape, a.dtype) for a in fou...]
where the time goes in v2:
time: 65.2 us; the launch traced here: 65 us
  Pallas kernels  64.4 us (99%)
    pallas_call x1, Pallas kernels, shards(): pl.pallas_call(functools.partial(kernel, 16384.0 ** (-0.5)), out_shape=(s...  62 us
    pallas_call x1, Pallas kernels, shards(): pl.pallas_call(write_out, out_shape=[shape(a.shape, a.dtype) for a in fou...  2.43 us

profile of v2, /device:TPU:1, one launch (start us, length us, event | category | flops | bytes accessed | tf_op | source)
XLA Modules:
  0.0 65.0 jit_solution(17055315273436397609)
XLA Ops:
  0.6 62.0 %layer_step.1 = (bf16[256,1024]{1,0:T(8,128)(2,1)}, bf16[256,512]{1,0:T(8,128)(2,1)}, bf16[256,512]{1,0:T(8,128)(2,1)}, bf16[256,512]{1,0:T(8,128)(2,1)}, f32[64,512]{1,0:T(8,128)}) custom-call(bf16[256,512]{1,0:T(8,128)(2,1)} %q_hbm.1, bf16[256,512]{1,0:T(8,128)(2,1)} %k_hbm.1, bf16[256,512]{1,0:T(8,128)(2,1)} %v_hbm.1, bf16[64,512]{1,0:T(8,128)(2,1)} %w_hbm.1, ...), custom_call_target="tpu_custom_call" | custom-call | tf_op jit(solution)/shard_map/layer_step/pallas_call | solution.py:555
  62.6 2.4 %write_out.1 = (bf16[256,1024]{1,0:T(8,128)(2,1)}, bf16[256,512]{1,0:T(8,128)(2,1)}, bf16[256,512]{1,0:T(8,128)(2,1)}, bf16[256,512]{1,0:T(8,128)(2,1)}, f32[64,512]{1,0:T(8,128)}) custom-call(bf16[256,1024]{1,0:T(8,128)(2,1)} %get-tuple-element.10.refs_0_, bf16[256,512]{1,0:T(8,128)(2,1)} %get-tuple-element.11.refs_1_, ...), custom_call_target="tpu_custom_call" | custom-call | tf_op jit(solution)/shard_map/write_out/pallas_call | solution.py:622

commit v3 on v2

--- a/solution.py
+++ b/solution.py
@@ -18,7 +18,8 @@
 EPS = 1e-06
 WROWS = 64
 WA = 16
-ARRIVALS = 84
+PARTS = 4
+ARRIVALS = 95
 DEPARTURES = 20
 MESH = pl.DeviceIdType.MESH
 f32 = jnp.float32
@@ -40,6 +41,7 @@
 def kernel(
     grad_scale,
     q_hbm, k_hbm, v_hbm, w_hbm, c_hbm,
+    lo_hbm, qg_hbm, kg_hbm, vg_hbm, dw_hbm,
     lo_ref, qg_ref, kg_ref, vg_ref, dw_ref,
     q_ref, k_ref, v_ref, qf, kf, scores, att, unit, inv, normed, datt, prior, kacc, vacc,
     state, own_b, sib_b, zsend, zrecv, tsend, trecv, psend, pre,
@@ -219,8 +221,8 @@
         block = wall.at[x, origin, c, part_b]
         return send(block, block, at(dz=way), "b")
 
-    def a_step(origin, way):
-        group = wall.at[:, origin, c, part_a]
+    def a_step(g, origin, way):
+        group = wall.at[pl.ds(2 * g, 2), origin, c, part_a]
         return send(group, group, at(dz=way), "a")
 
     bm = [b_step(z, s)]
@@ -243,7 +245,7 @@
         return send(call.at[b], csib.at[b], at(dc=1), "cot2")
 
     cot_c = {0: cot_share(y)}
-    am, ao = [], []
+    am, ao = ([], []), ([], [])
 
     def serve_b(i):
         bm[i].wait_recv()
@@ -257,22 +259,28 @@
 
     def serve_a0():
         await_all(wall.at[pl.ds(0, NX - 1), 0, 0, part_a], xa)
-        am.append(a_step(z, s))
-        ao.append(a_step(z, -s))
+        for g in (0, 1):
+            am[g].append(a_step(g, z, s))
+            ao[g].append(a_step(g, z, -s))
 
     def serve_a(i):
-        am[i].wait_recv()
-        if i < 3:
-            am.append(a_step(place(i + 1), s))
-            ao[i].wait_recv()
-            if i < 2:
-                ao.append(a_step(place(-i - 1), -s))
+        for g in (0, 1):
+            am[g][i].wait_recv()
+            if i < 3:
+                am[g].append(a_step(g, place(i + 1), s))
+                ao[g][i].wait_recv()
+                if i < 2:
+                    ao[g].append(a_step(g, place(-i - 1), -s))
 
     wsib = arrival()
 
-    def share_w(k):
+    def share_b(k):
         await_all(wall.at[0, 0, 0, part_b], xr[k])
-        group = wall.at[:, place(k), c]
+        group = wall.at[:, place(k), c, part_b]
+        send(group, group, at(dc=1), "wshare", wsib)
+
+    def share_a():
+        group = wall.at[:, :, c, part_a]
         send(group, group, at(dc=1), "wshare", wsib)
 
     def intra(h):
@@ -289,26 +297,31 @@
     b_relay(0)
     scan = scan_total(0, scan, False)
     serve_b(1)
+    serve_a(0)
     b_relay(1)
     b_relay(-1)
-    serve_a(0)
     p_top.wait_recv()
     f_top = cot(down_y, top, 1)
     m_bottom.wait_recv()
     f_bottom = cot(up_y, bottom, -1)
     scan = scan_back(0, scan, False)
     serve_b(2)
+    serve_a(1)
     b_relay(2)
     b_relay(-2)
-    serve_a(1)
-    share_w(0)
+    share_b(0)
     serve_b(3)
+    serve_a(2)
+    m_top.wait_recv()
+    cot_c[1] = cot_share(up_y)
     b_relay(3)
     b_relay(-3)
+    share_b(1)
+    share_b(-1)
     scan = scan_share(0, scan)
-    serve_a(2)
-    share_w(1)
-    share_w(-1)
+    p_bottom.wait_recv()
+    cot_c[3] = cot_share(down_y)
+    b_relay(4)
     scan_end(0, scan, False)
 
     for h in range(HEADS):
@@ -325,16 +338,12 @@
         ntsend[h // 2, pl.ds((h % 2) * HD, HD), :] = t
     nt_copy = send(ntsend.at[1 - c], ntsib, at(dc=1), "nt")
     ntown[...] = ntsend[c]
-    m_top.wait_recv()
-    cot_c[1] = cot_share(up_y)
-    b_relay(4)
-    share_w(2)
-    share_w(-2)
+    share_b(2)
+    share_b(-2)
     serve_a(3)
-    p_bottom.wait_recv()
-    cot_c[3] = cot_share(down_y)
-
-    half_rows = HD // 2
+    share_a()
+
+    part_rows = HD // PARTS
 
     def products(j):
         b = lax.rem(y + j, NY)
@@ -343,11 +352,16 @@
         for o in range(NZ):
             lanes = slice(o * HD, (o + 1) * HD)
             pz[j, o] = p[:HD, lanes]
-            xsend[0, j, o] = p[HD : HD + half_rows, lanes].astype(bf16)
-            xsend[1, j, o] = p[HD + half_rows :, lanes].astype(bf16)
+            for g in range(PARTS):
+                low = HD + g * part_rows
+                xsend[g, j, o] = p[low : low + part_rows, lanes].astype(bf16)
 
     rm, ro = ([], []), ([], [])
-    groups = ((0, 1), (3, 2))
+    groups = ((0, 1, 3), (2,))
+
+    def ring_send(g, i, way):
+        count = pl.ds(0, len(groups[g]))
+        return send(rsend.at[g, i, count], rrecv.at[g, i, count], at(dz=way), "ring")
 
     def ring(g, i):
         if i:
@@ -358,7 +372,7 @@
             if i:
                 p = p + rrecv[g, i - 1, n].astype(f32)
             rsend[g, i, n] = p.astype(bf16)
-        rm[g].append(send(rsend.at[g, i], rrecv.at[g, i], at(dz=s), "ring"))
+        rm[g].append(ring_send(g, i, s))
         if i < 3:
             if i:
                 ro[g][i - 1].wait_recv()
@@ -368,7 +382,7 @@
                 if i:
                     p = p + rrecv[g, 4 + i - 1, n].astype(f32)
                 rsend[g, 4 + i, n] = p.astype(bf16)
-            ro[g].append(send(rsend.at[g, 4 + i], rrecv.at[g, 4 + i], at(dz=-s), "ring"))
+            ro[g].append(ring_send(g, 4 + i, -s))
 
     def ring_end(g):
         rm[g][3].wait_recv()
@@ -403,19 +417,18 @@
     nt_copy.wait_recv()
     products(0)
     products(1)
+    products(3)
     ring(0, 0)
-    products(3)
-    share_w(3)
-    share_w(-3)
-    share_w(4)
-
     f_top.wait_recv()
     f_bottom.wait_recv()
     cot_c[2] = cot_share(far_y)
+    share_b(3)
+    share_b(-3)
+    share_b(4)
     products(2)
+    xs = [x_send(0)]
     ring(1, 0)
-    x0 = x_send(0)
-    x1 = x_send(1)
+    xs += [x_send(g) for g in range(1, PARTS)]
 
     def weight(b):
         return wall[b].reshape(FEATS, WIDTH)
@@ -470,20 +483,37 @@
     ring(0, 2)
     for h in range(HEADS):
         grads(h)
+    outs = [load(0, qg_ref, qg_hbm)]
+    ds = [x_sum(0, xs[0])]
+    ring(1, 2)
     scan = scan_total(1, scan, True)
-    ring(1, 2)
+    ring(0, 3)
+    ds.append(x_sum(1, xs[1]))
     layer_pass()
-    ring(0, 3)
-    d0 = x_sum(0, x0)
     ring(1, 3)
+    ds.append(x_sum(2, xs[2]))
     scan = scan_back(1, scan, True)
     ring_end(0)
-    d1 = x_sum(1, x1)
     ring_end(1)
     landed_e = arrival()
     for j in range(1, NX):
         send(esend.at[place_of(j)], erecv.at[j - 1], at(dx=j), "e", landed_e)
+    ds.append(x_sum(3, xs[3]))
     scan = scan_share(1, scan)
+    await_all(erecv, landed_e)
+    t = zown[place_of(0)]
+    for j in range(NX - 1):
+        t = t + erecv[j].astype(f32)
+    mine[:, pl.ds(0, HD)] = t.T
+    for g, landed in enumerate(ds):
+        await_all(drecv.at[g], landed)
+        t = xsum[g, z]
+        for j in range(NZ - 1):
+            t = t + drecv[g, j].astype(f32)
+        xsum[g, z] = t
+    mine[:, pl.ds(HD, HD)] = jnp.concatenate([xsum[g, z] for g in range(PARTS)], axis=0).T
+    other = pl.multiple_of((1 - c) * WROWS, WROWS)
+    last = send(mine.at[pl.ds(other, WROWS)], tsib_recv, at(dc=1), "last")
     scan_end(1, scan, True)
     for h in range(HEADS):
         st = state[rows(h), :].astype(bf16)
@@ -491,28 +521,17 @@
         kg_ref[:, cols(h)] = (kg * slope(k_ref, h)).astype(bf16)
         vg_ref[:, cols(h)] = (vacc[:, cols(h)] + nn(kf[:, cols(h)], st)).astype(bf16)
 
+    outs += [load(1, kg_ref, kg_hbm), load(2, vg_ref, vg_hbm)]
     await_all(lrecv, near)
     lo_ref[...] = (lout[2] + lrecv[0].astype(f32) + lrecv[1].astype(f32)).astype(bf16)
 
-    await_all(erecv, landed_e)
-    t = zown[place_of(0)]
-    for j in range(NX - 1):
-        t = t + erecv[j].astype(f32)
-    mine[:, pl.ds(0, HD)] = t.T
-    for g, landed in enumerate((d0, d1)):
-        await_all(drecv.at[g], landed)
-        t = xsum[g, z]
-        for j in range(NZ - 1):
-            t = t + drecv[g, j].astype(f32)
-        xsum[g, z] = t
-    mine[:, pl.ds(HD, HD)] = jnp.concatenate([xsum[0, z], xsum[1, z]], axis=0).T
-    other = pl.multiple_of((1 - c) * WROWS, WROWS)
-    last = send(mine.at[pl.ds(other, WROWS)], tsib_recv, at(dc=1), "last")
+    outs.append(load(3, lo_ref, lo_hbm))
     last.wait_recv()
     here = mine[pl.ds(pl.multiple_of(c * WROWS, WROWS), WROWS), :] * grad_scale
     there = tsib_recv[...] * grad_scale
     dw_ref[:, pl.ds(0, 2 * HD)] = jnp.where(c == 0, here, there)
     dw_ref[:, pl.ds(2 * HD, 2 * HD)] = jnp.where(c == 0, there, here)
+    outs.append(load(4, dw_ref, dw_hbm))
     sent("own", own_b)
     sent("chip", zrecv.at[:, pl.ds(0, NZ - 1)])
     sent("total", trecv.at[:, pl.ds(0, NX - 1)])
@@ -528,20 +547,30 @@
     sent("cot2", call)
     sent("nt", ntsib)
     sent("layer", lsend)
-    sent("ring", rsend)
+    sent("ring", rsend.at[:, :, pl.ds(0, 2)])
     sent("x", xrecv)
     sent("d", drecv)
     sent("e", erecv)
     sent("last", tsib_recv)
+    for copy in outs:
+        copy.wait()
     assert not kinds and len(arrivals) == ARRIVALS
 
 
 def write_out(*refs):
-    sem = refs[-1]
-    copies = [pltpu.make_async_copy(refs[i], refs[5 + i], sem.at[i]) for i in range(5)]
-    for copy in copies:
+    ins, outs, bufs, (here, there) = refs[:5], refs[5:10], refs[10:15], refs[15:]
+
+    def start(i, src, dst, sem):
+        copy = pltpu.make_async_copy(src, dst, sem.at[i])
         copy.start()
-    for copy in copies:
+        return copy
+
+    coming = [start(i, ins[i], bufs[i], here) for i in range(5)]
+    going = []
+    for i in (4, 1, 2, 3, 0):
+        coming[i].wait()
+        going.append(start(i, bufs[i], outs[i], there))
+    for copy in going:
         copy.wait()
 
 
@@ -562,8 +591,13 @@
                 shape((WROWS, WIDTH), f32),
             ),
             in_specs=[pl.BlockSpec(memory_space=pltpu.HBM)] * 5,
-            out_specs=[pl.BlockSpec(memory_space=pltpu.VMEM)] * 5,
+            out_specs=[pl.BlockSpec(memory_space=pltpu.HBM)] * 5,
             scratch_shapes=[
+                vm((ROWS, FEATS), bf16),
+                vm((ROWS, WIDTH), bf16),
+                vm((ROWS, WIDTH), bf16),
+                vm((ROWS, WIDTH), bf16),
+                vm((WROWS, WIDTH), f32),
                 vm((ROWS, WIDTH), bf16),
                 vm((ROWS, WIDTH), bf16),
                 vm((ROWS, WIDTH), bf16),
@@ -598,13 +632,13 @@
                 vm((2, 2 * HD, ROWS), bf16),
                 vm((2 * HD, ROWS), bf16),
                 vm((NX, NZ, HD, HD), f32),
-                vm((2, NX, NZ, HD // 2, HD), bf16),
-                vm((2, NX - 1, NZ, HD // 2, HD), bf16),
-                vm((2, NZ, HD // 2, HD), f32),
-                vm((2, NZ, HD // 2, HD), bf16),
-                vm((2, NZ - 1, HD // 2, HD), bf16),
-                vm((2, 7, 2, HD, HD), bf16),
-                vm((2, 7, 2, HD, HD), bf16),
+                vm((PARTS, NX, NZ, HD // PARTS, HD), bf16),
+                vm((PARTS, NX - 1, NZ, HD // PARTS, HD), bf16),
+                vm((PARTS, NZ, HD // PARTS, HD), f32),
+                vm((PARTS, NZ, HD // PARTS, HD), bf16),
+                vm((PARTS, NZ - 1, HD // PARTS, HD), bf16),
+                vm((2, 7, 3, HD, HD), bf16),
+                vm((2, 7, 3, HD, HD), bf16),
                 vm((NX, HD, HD), f32),
                 vm((NX, HD, HD), bf16),
                 vm((NX - 1, HD, HD), bf16),
@@ -622,9 +656,13 @@
         return pl.pallas_call(
             write_out,
             out_shape=[shape(a.shape, a.dtype) for a in found],
-            in_specs=[pl.BlockSpec(memory_space=pltpu.VMEM)] * 5,
+            in_specs=[pl.BlockSpec(memory_space=pltpu.HBM)] * 5,
             out_specs=[pl.BlockSpec(memory_space=pltpu.HBM)] * 5,
-            scratch_shapes=[pltpu.SemaphoreType.DMA((5,))],
+            scratch_shapes=[
+                *(vm(a.shape, a.dtype) for a in found),
+                pltpu.SemaphoreType.DMA((5,)),
+                pltpu.SemaphoreType.DMA((5,)),
+            ],
             name="write_out",
         )(*found)
 

time: 65.2 us -> 63.2 us (0.969)
  Pallas kernels: 64.4 us -> 62.4 us
    pallas_call x1, Pallas kernels: 62 us -> 59.9 us  [shards(): pl.pallas_call(functools.partial(kernel, 16384.0 ** (-0.5)), out_shape=(s...]
where the time goes in v3:
time: 63.2 us; the launch traced here: 63 us
  Pallas kernels  62.4 us (99%)
  between operations  0.64 us (1%)
    pallas_call x1, Pallas kernels, shards(): pl.pallas_call(functools.partial(kernel, 16384.0 ** (-0.5)), out_shape=(s...  59.9 us
    pallas_call x1, Pallas kernels, shards(): pl.pallas_call(write_out, out_shape=[shape(a.shape, a.dtype) for a in fou...  2.48 us

profile of v3, /device:TPU:1, one launch (start us, length us, event | category | flops | bytes accessed | tf_op | source)
XLA Modules:
  0.0 63.0 jit_solution(1703154995018881612)
XLA Ops:
  0.6 59.9 %layer_step.1 = (bf16[256,1024]{1,0:T(8,128)(2,1)}, bf16[256,512]{1,0:T(8,128)(2,1)}, bf16[256,512]{1,0:T(8,128)(2,1)}, bf16[256,512]{1,0:T(8,128)(2,1)}, f32[64,512]{1,0:T(8,128)}) custom-call(bf16[256,512]{1,0:T(8,128)(2,1)} %q_hbm.1, bf16[256,512]{1,0:T(8,128)(2,1)} %k_hbm.1, bf16[256,512]{1,0:T(8,128)(2,1)} %v_hbm.1, bf16[64,512]{1,0:T(8,128)(2,1)} %w_hbm.1, ...), custom_call_target="tpu_custom_call" | custom-call | tf_op jit(solution)/shard_map/layer_step/pallas_call | solution.py:584
  60.6 2.5 %write_out.1 = (bf16[256,1024]{1,0:T(8,128)(2,1)}, bf16[256,512]{1,0:T(8,128)(2,1)}, bf16[256,512]{1,0:T(8,128)(2,1)}, bf16[256,512]{1,0:T(8,128)(2,1)}, f32[64,512]{1,0:T(8,128)}) custom-call(bf16[256,1024]{1,0:T(8,128)(2,1)} %get-tuple-element.10.refs_0_, bf16[256,512]{1,0:T(8,128)(2,1)} %get-tuple-element.11.refs_1_, ...), custom_call_target="tpu_custom_call" | custom-call | tf_op jit(solution)/shard_map/write_out/pallas_call | solution.py:656

commit v4 on v3

--- a/solution.py
+++ b/solution.py
@@ -414,6 +414,9 @@
             send(dsend.at[g, zat(j)], drecv.at[g, j - 1], at(dz=j), "d", landed)
         return landed
 
+    share_b(3)
+    share_b(-3)
+    share_b(4)
     nt_copy.wait_recv()
     products(0)
     products(1)
@@ -422,9 +425,6 @@
     f_top.wait_recv()
     f_bottom.wait_recv()
     cot_c[2] = cot_share(far_y)
-    share_b(3)
-    share_b(-3)
-    share_b(4)
     products(2)
     xs = [x_send(0)]
     ring(1, 0)

time: 63.2 us -> 63.3 us (level)
  no operation moved by 1% of the time
where the time goes in v4:
time: 63.3 us; the launch traced here: 63.2 us
  Pallas kernels  62.6 us (99%)
  between operations  0.64 us (1%)
    pallas_call x1, Pallas kernels, shards(): pl.pallas_call(functools.partial(kernel, 16384.0 ** (-0.5)), out_shape=(s...  60.1 us
    pallas_call x1, Pallas kernels, shards(): pl.pallas_call(write_out, out_shape=[shape(a.shape, a.dtype) for a in fou...  2.48 us

profile of v4, /device:TPU:1, one launch (start us, length us, event | category | flops | bytes accessed | tf_op | source)
XLA Modules:
  0.0 63.2 jit_solution(5123839401469923866)
XLA Ops:
  0.6 60.1 %layer_step.1 = (bf16[256,1024]{1,0:T(8,128)(2,1)}, bf16[256,512]{1,0:T(8,128)(2,1)}, bf16[256,512]{1,0:T(8,128)(2,1)}, bf16[256,512]{1,0:T(8,128)(2,1)}, f32[64,512]{1,0:T(8,128)}) custom-call(bf16[256,512]{1,0:T(8,128)(2,1)} %q_hbm.1, bf16[256,512]{1,0:T(8,128)(2,1)} %k_hbm.1, bf16[256,512]{1,0:T(8,128)(2,1)} %v_hbm.1, bf16[64,512]{1,0:T(8,128)(2,1)} %w_hbm.1, ...), custom_call_target="tpu_custom_call" | custom-call | tf_op jit(solution)/shard_map/layer_step/pallas_call | solution.py:584
  60.7 2.5 %write_out.1 = (bf16[256,1024]{1,0:T(8,128)(2,1)}, bf16[256,512]{1,0:T(8,128)(2,1)}, bf16[256,512]{1,0:T(8,128)(2,1)}, bf16[256,512]{1,0:T(8,128)(2,1)}, f32[64,512]{1,0:T(8,128)}) custom-call(bf16[256,1024]{1,0:T(8,128)(2,1)} %get-tuple-element.10.refs_0_, bf16[256,512]{1,0:T(8,128)(2,1)} %get-tuple-element.11.refs_1_, ...), custom_call_target="tpu_custom_call" | custom-call | tf_op jit(solution)/shard_map/write_out/pallas_call | solution.py:656
